TPU v7x, 256 devices: a whole 4x4x8 slice. The times are simulated.
256 devices in a mesh: pair: 16 (over x_lo, y, core), grp: 16 (over z, x_hi).
Axes of the slice: x: 4 (x_hi: 2, x_lo: 2; x = x_hi * 2 + x_lo), y: 4, z: 8, core: 2. Of those that a mesh axis runs over, the one named last changes fastest.
Arguments:
- amplitudes: float32 [48, 48, 4096], P('pair', 'grp'), may hold values from -6 to 6
- integrals: float32 [4096, 20480], P('pair', 'grp'), may hold values from -0.125 to 0.125
- occ_start: int32 [8], replicated, may hold values from 0 to 2160, as said below
- vir_start: int32 [8], replicated, may hold values from 0 to 3840, as said below
- block_mask: int32 [8, 8], replicated, may hold values 0 or 1
- occ_energy: float32 [48, 48], P('pair', 'grp'), may hold values from -1.5 to -0.5
- vir_energy: float32 [20480], replicated, may hold values from 0.4 to 2.5
Outputs:
- update: float32 [48, 48, 20480], P('pair', 'grp')
Inputs may be any that keep to these rules, and one draw needn't show every extreme that they name: `occ_start`: strictly rising; the first entry is 0; the last block holds 144 pairs. `vir_start`: strictly rising; the first entry is 0; the last block holds 256 pairs.
All inputs are finite; a program needn't handle non-finite values.
Results may differ from a plain program's by a relative error of at most 0.00007.
Values sent between devices are 32-bit elements; how exact they have to be, the bound alone decides.
No kernel may reach another device: no remote copies, remote signals or barrier semaphores. Data moves between devices by JAX's collectives and lax.ppermute only.
A program may use at most 128 MiB of HBM per device.

v0:
```python
import jax
import jax.numpy as jnp
from jax import lax
from jax.sharding import PartitionSpec as P


def block_ids(index, starts):
    return jnp.sum((index[:, None] >= starts[None, :]).astype(jnp.int32), axis=1) - 1


def mask_rows(values, row_ids, col_ids, occ_start, vir_start, block_mask):
    row_hot = (
        block_ids(row_ids, occ_start)[:, None]
        == jnp.arange(occ_start.shape[0], dtype=jnp.int32)[None, :]
    ).astype(jnp.float32)
    col_hot = (
        block_ids(col_ids, vir_start)[:, None]
        == jnp.arange(vir_start.shape[0], dtype=jnp.int32)[None, :]
    ).astype(jnp.float32)
    row_keep = jnp.dot(
        row_hot,
        block_mask.astype(jnp.float32),
        precision=lax.Precision.HIGHEST,
        preferred_element_type=jnp.float32,
    )
    keep = jnp.dot(
        row_keep, col_hot.T, precision=lax.Precision.HIGHEST, preferred_element_type=jnp.float32
    )
    return values * keep


def on_device(amplitudes, integrals, occ_start, vir_start, block_mask, occ_energy, vir_energy):
    pair_pos = lax.axis_index("pair")
    grp_pos = lax.axis_index("grp")
    groups = lax.axis_size("grp")
    moved = lax.all_to_all(amplitudes, "pair", split_axis=2, concat_axis=0, tiled=True)
    outer, inner, width = moved.shape
    inner_ids = grp_pos * inner + jnp.arange(inner, dtype=jnp.int32)
    outer_ids = jnp.arange(outer, dtype=jnp.int32) * (inner * groups)
    row_ids = (outer_ids[:, None] + inner_ids[None, :]).reshape(-1)
    col_ids = pair_pos * width + jnp.arange(width, dtype=jnp.int32)
    flat = mask_rows(
        moved.reshape(outer * inner, width), row_ids, col_ids, occ_start, vir_start, block_mask
    )
    piece = lax.all_gather(integrals, "grp", axis=1, tiled=True)
    product = jnp.dot(
        flat, piece, precision=lax.Precision.HIGHEST, preferred_element_type=jnp.float32
    )
    partial_value = product.reshape(outer, inner, piece.shape[1])
    ladder = lax.psum_scatter(partial_value, "pair", scatter_dimension=0, tiled=True)
    denom = occ_energy[:, :, None] - vir_energy[None, None, :]
    return ladder / denom


def solution(mesh):
    return jax.shard_map(
        on_device,
        mesh=mesh,
        in_specs=(P("pair", "grp", None), P("pair", "grp"), P(), P(), P(), P("pair", "grp"), P()),
        out_specs=P("pair", "grp", None),
        check_vma=False,
    )
```

profile of v0, /device:TPU:2, one launch (start us, length us, event | category | flops | bytes accessed | tf_op | source)
XLA Modules:
  0.0 514.3 jit_solution(2934326912235342113)
XLA Ops:
  6.5 0.0 copy-start.2
  6.5 0.0 all-gather.2.cloned.1.call-start
  6.5 0.7 all-gather.2.cloned.1.call-update
  7.3 6.6 %copy.11 = f32[3,3,4096]{1,0,2:T(4,128)} copy(f32[3,3,4096]{2,1,0:T(4,128)} %param.7) | data formatting | bytes 294912 | tf_op args[0]
  13.8 9.3 %reshape.46 = f32[16,1,2304]{2,1,0:T(1,128)} reshape(f32[4096,3,3]{2,1,0:T(4,128)} %bitcast.9) | data formatting | bytes 294912
  23.1 5.9 %all-to-all-start = ((f32[16,1,2304]{2,1,0:T(1,128)}), f32[16,1,2304]{2,1,0:T(1,128)S(1)}, u32[]{:S(2)}, u32[]{:S(2)}) async-start(f32[16,1,2304]{2,1,0:T(1,128)} %reshape.46), calls=%async_computation | async-start | bytes 294912 | tf_op jit(solution)/shard_map/all_to_all | solution.py:36
  29.1 0.0 all-reduce.3.cloned.1.call-start
  29.2 0.1 broadcast_add_fusion
  29.2 0.1 add.57
  29.4 0.0 copy-done.2
  29.4 0.1 convert_reduce_fusion.1
  29.5 0.0 copy-done.3
  29.5 0.1 convert_reduce_fusion
  29.6 0.0 copy-done.4
  29.6 0.2 fusion
  29.8 6.7 %all-to-all-done = f32[16,1,2304]{2,1,0:T(1,128)S(1)} async-done(((f32[16,1,2304]{2,1,0:T(1,128)}), f32[16,1,2304]{2,1,0:T(1,128)S(1)}, u32[]{:S(2)}, u32[]{:S(2)}) %all-to-all-start) | async-done | bytes 147488 | tf_op jit(solution)/shard_map/all_to_all | solution.py:36
  36.4 0.5 broadcast.38
  36.9 1.0 reduce
  37.9 6.8 %reshape.47 = f32[4096,3,3]{2,1,0:T(4,128)} reshape(f32[16,2304]{1,0:T(8,128)S(1)} %reduce) | data formatting | bytes 294912
  44.7 6.6 %copy.12 = f32[3,3,16,256]{3,1,0,2:T(4,128)S(1)} copy(f32[3,3,16,256]{1,0,3,2:T(4,128)} %bitcast.8) | data formatting | bytes 294912 | tf_op jit(solution)/shard_map/all_to_all | solution.py:36
  51.3 0.1 reshape.43
  51.4 0.3 convolution_multiply_fusion
  51.7 234.0 %all-gather.2.cloned.1.call-done = f32[256,20480]{1,0:T(8,128)} async-done(((f32[256,1280]{1,0:T(8,128)}), f32[256,20480]{1,0:T(8,128)}) %all-gather.2.cloned.1.call-update) | async-done | bytes 20971536 | tf_op jit(solution)/shard_map/all_gather | solution.py:45
  285.7 19.1 %fusion.4 = f32[144,20480]{1,0:T(8,128)} fusion(f32[144,256]{1,0:T(8,128)S(1)} %convolution_multiply_fusion, f32[256,20480]{1,0:T(8,128)} %all-gather.2.cloned.1.call-done), kind=kOutput, calls=%fused_computation.16 | convolution fusion | flops 9059696640 | bytes 32915456 | tf_op jit(solution)/shard_map/dot_general | solution.py:46
  304.8 12.7 %reshape.44 = f32[48,3,20480]{2,1,0:T(4,128)} reshape(f32[144,20480]{1,0:T(8,128)} %fusion.4) | data formatting | bytes 23592960 | tf_op jit(solution)/shard_map/reshape | solution.py:49
  317.5 0.0 all-reduce.3.cloned.1.call-update
  317.5 0.0 copy-done.5
  317.5 0.6 dynamic-slice
  318.7 186.2 %all-reduce.3.cloned.1.call-done = f32[48,3,20480]{2,1,0:T(4,128)} async-done(((f32[48,3,20480]{2,1,0:T(4,128)}), f32[48,3,20480]{2,1,0:T(4,128)}) %all-reduce.3.cloned.1.call-update) | async-done | bytes 11796496
  505.0 0.0 copy-done
  505.0 0.0 copy-done.1
  505.0 2.5 dynamic-slice_divide_fusion
  (10 shorter events, 0.0 us)
Async XLA Ops:
  6.5 22.8 %copy-start.2 = (s32[8]{0:T(128)S(1)}, s32[8]{0:T(128)}, u32[]{:S(2)}) copy-start(s32[8]{0:T(128)} %param.9) | copy-start | bytes 100
  6.5 22.9 %copy-start.3 = (s32[8]{0:T(128)S(1)}, s32[8]{0:T(128)}, u32[]{:S(2)}) copy-start(s32[8]{0:T(128)} %param.10) | copy-start | bytes 100
  6.5 23.0 %copy-start.4 = (s32[8,8]{1,0:T(8,128)S(1)}, s32[8,8]{1,0:T(8,128)}, u32[]{:S(2)}) copy-start(s32[8,8]{1,0:T(8,128)} %param.11) | copy-start | bytes 772
  6.5 279.1 %all-gather.2.cloned.1.call-start = ((), (), s32[]{:S(2)}) async-start(), calls=%async_computation.1 | async-start | bytes 22282240 | tf_op jit(solution)/shard_map/all_gather | solution.py:45
  23.1 13.3 %all-to-all-start = ((f32[16,1,2304]{2,1,0:T(1,128)}), f32[16,1,2304]{2,1,0:T(1,128)S(1)}, u32[]{:S(2)}, u32[]{:S(2)}) async-start(f32[16,1,2304]{2,1,0:T(1,128)} %reshape.46), calls=%async_computation | async-start | bytes 294912 | tf_op jit(solution)/shard_map/all_to_all | solution.py:36
  29.1 475.9 %all-reduce.3.cloned.1.call-start = ((), (), s32[]{:S(2)}) async-start(), calls=%async_computation.2 | async-start | bytes 31457280
  304.8 12.7 %copy-start.5 = (u32[256]{0:T(256)S(1)}, u32[256]{0:T(256)}, u32[]{:S(2)}) copy-start(u32[256]{0:T(256)} %constant.24) | copy-start | bytes 3076
  304.8 200.2 %copy-start = (f32[20480]{0:T(1024)S(1)}, f32[20480]{0:T(1024)}, u32[]{:S(2)}) copy-start(f32[20480]{0:T(1024)} %param.13) | copy-start | bytes 245764
  304.8 200.2 %copy-start.1 = (f32[3,3]{1,0:T(4,128)S(1)}, f32[3,3]{1,0:T(4,128)}, u32[]{:S(2)}) copy-start(f32[3,3]{1,0:T(4,128)} %param.12) | copy-start | bytes 112
Sparse Core Ops, SparseCore 0:
  10.0 275.6 all-gather.1
  317.6 187.3 all-reduce.2
where the time goes:
time: 516 us; the launch traced here: 514 us
  waiting for transfers between devices  428 us (83%)
  local copies, waits for them, and re-layouts  43.2 us (8%)
  matrix products  19.6 us (4%)
  between operations  14.1 us (3%)
  starting transfers between devices  5.99 us (1%)
    all_gather x1, waiting for transfers between devices, on_device(): piece = lax.all_gather(integrals, 'grp', axis=1, tiled=True)  234 us
    unnamed x3, waiting for transfers between devices  187 us
    unnamed x16, local copies, waits for them, and re-layouts  23.2 us
    dot_general x1, matrix products, on_device(): jnp.dot(flat, piece, precision=lax.Precision.HIGHEST, preferred_element_t...  19.1 us
    reshape x1, local copies, waits for them, and re-layouts, on_device(): partial_value = product.reshape(outer, inner, piece.shape[1])  12.7 us
  transfers between devices with their start and end apart: 3, of which 3 were waited for; matrix products, arithmetic and copies ran while one was open for 6% of the time, Pallas kernels for 0%

commit v1 on v0

v1 whole, which is shorter than its diff:
```python
import jax
import jax.numpy as jnp
from jax import lax
from jax.experimental import pallas as pl
from jax.experimental.pallas import tpu as pltpu
from jax.sharding import Mesh, PartitionSpec as P

AXES = ("xl", "y", "core", "z", "xh")
SIZES = (2, 4, 2, 8, 2)
PAIR, GRP = ("xl", "y", "core"), ("z", "xh")
NZ = 8


def swap(x, axes, bits):
    names = axes if isinstance(axes, tuple) else (axes,)
    n = 1
    for a in names:
        n *= SIZES[AXES.index(a)]
    return lax.ppermute(x, axes, [(i, i ^ bits) for i in range(n)])


def along_z(x, d):
    return lax.ppermute(x, "z", [(i, (i + d) % NZ) for i in range(NZ)])


def mask_kernel(occ_ref, vir_ref, mask_ref, a_ref, out_ref, held):
    xl, y, core = lax.axis_index("xl"), lax.axis_index("y"), lax.axis_index("core")
    z, xh = lax.axis_index("z"), lax.axis_index("xh")
    no, ni, width = a_ref.shape
    blocks = vir_ref.shape[0]
    part = width // 16
    col = lax.broadcasted_iota(jnp.int32, (1, width), 1)
    block = jnp.full((1, width), -1, jnp.int32)
    for s in range(blocks):
        block = block + (col >= vir_ref[s]).astype(jnp.int32)
    for oo in range(no):
        for ii in range(ni):
            o = ((xl * 4 + y) * 2 + core) * no + oo
            row = o * (ni * 16) + (z * 2 + xh) * ni + ii
            row_block = jnp.int32(-1)
            for s in range(occ_ref.shape[0]):
                row_block = row_block + (row >= occ_ref[s]).astype(jnp.int32)
            keep = jnp.zeros((1, width), jnp.float32)
            for v in range(blocks):
                keep = jnp.where(block == v, mask_ref[row_block, v].astype(jnp.float32), keep)
            held[oo * ni + ii : oo * ni + ii + 1, :] = a_ref[oo, ii : ii + 1, :] * keep
    for e in range(4):
        for dc in range(2):
            for dx in range(2):
                p = ((xl ^ dx) * 4 + (y ^ e)) * 2 + (core ^ dc)
                out_ref[dc, e, :, dx * part : (dx + 1) * part] = held[
                    :, pl.ds(pl.multiple_of(p * part, part), part)
                ]


def mask_rows(amplitudes, occ_start, vir_start, block_mask):
    no, ni, width = amplitudes.shape
    smem = pl.BlockSpec(memory_space=pltpu.SMEM)
    vmem = pl.BlockSpec(memory_space=pltpu.VMEM)
    return pl.pallas_call(
        mask_kernel,
        out_shape=jax.ShapeDtypeStruct((2, 4, no * ni, width // 8), jnp.float32),
        in_specs=[smem, smem, smem, vmem],
        out_specs=vmem,
        scratch_shapes=[pltpu.VMEM((no * ni, width), jnp.float32)],
    )(occ_start, vir_start, block_mask, amplitudes)


def scale_kernel(*refs):
    parts, (occ_ref, vir_ref, out_ref) = refs[:NZ], refs[NZ:]
    z, xh = lax.axis_index("z"), lax.axis_index("xh")
    width = parts[0].shape[2] // 2
    for d in range(NZ):
        for h in range(2):
            where = (lax.rem(z + d, NZ) * 2 + (xh ^ h)) * width
            cols = pl.ds(pl.multiple_of(where, width), width)
            for oo in range(out_ref.shape[0]):
                denom = occ_ref[oo] - vir_ref[:, cols]
                out_ref[oo, :, cols] = parts[d][oo, :, h * width : (h + 1) * width] / denom


def scale(parts, occ_energy, vir_energy):
    no, ni, width = parts[0].shape
    vmem = pl.BlockSpec(memory_space=pltpu.VMEM)
    return pl.pallas_call(
        scale_kernel,
        out_shape=jax.ShapeDtypeStruct((no, ni, width * NZ), jnp.float32),
        in_specs=[vmem] * (NZ + 2),
        out_specs=vmem,
    )(*parts, occ_energy[:, :, None], vir_energy[None, :])


def dot(a, b):
    return jnp.dot(a, b, precision=lax.Precision.HIGH, preferred_element_type=jnp.float32)


def on_device(amplitudes, integrals, occ_start, vir_start, block_mask, occ_energy, vir_energy):
    no, ni, _ = amplitudes.shape
    nr = no * ni
    with jax.named_scope("gather_integrals"):
        b_xl = swap(integrals, "xl", 1)
        b_d = swap(integrals, ("xl", "xh"), 3)
        b_xh = swap(integrals, "xh", 1)
    with jax.named_scope("mask"):
        sends = mask_rows(amplitudes, occ_start, vir_start, block_mask)
    depth = sends.shape[3]
    with jax.named_scope("exchange_amplitudes"):
        pair = jnp.stack([sends[0], swap(sends[1], "core", 1)], axis=1)
        rows = [pair[0]] + [swap(pair[e], "y", e) for e in (1, 2, 3)]
        mine = jnp.stack(rows, axis=1).reshape(8 * nr, depth)
    with jax.named_scope("gather_amplitudes"):
        got = [mine] + [along_z(mine, d) for d in range(1, NZ)]
        flat = jnp.stack([g.reshape(2, 4, nr, depth) for g in got], axis=2)
        flat = flat.reshape(2, 4 * NZ * nr, depth)
    half = depth // 2
    group = NZ * nr

    def block(side, h):
        near, far = ((integrals, b_xl), (b_xh, b_d))[h]
        return dot(flat[side, :, :half], near) + dot(flat[side, :, half:], far)

    sums = []
    for h in range(2):
        with jax.named_scope("product"):
            theirs = block(1, h)
        with jax.named_scope("sum_core"):
            other = swap(theirs, "core", 1)
        with jax.named_scope("product"):
            total = block(0, h)
        with jax.named_scope("sum_core"):
            total = (total + other).reshape(4, group, -1)
        sums.append(total)
    with jax.named_scope("sum_y"):
        r0 = swap(sums[0][1:3], "y", 1)
        r1 = swap(sums[1][2:4], "y", 3)
        s0 = swap(sums[0][3] + r0[1], "y", 3)
        s1 = swap(sums[1][1] + r1[0], "y", 1)
        piece = jnp.concatenate([sums[0][0] + r0[0] + s0, sums[1][0] + r1[1] + s1], axis=1)
    with jax.named_scope("to_owner"):
        piece = piece.reshape(NZ, no, ni, -1)
        parts = [piece[0]] + [along_z(piece[d], NZ - d) for d in range(1, NZ)]
    with jax.named_scope("scale"):
        return scale(parts, occ_energy, vir_energy)


def solution(mesh):
    split = Mesh(mesh.devices.reshape(SIZES), AXES)
    return jax.shard_map(
        on_device,
        mesh=split,
        in_specs=(P(PAIR, GRP, None), P(PAIR, GRP), P(), P(), P(), P(PAIR, GRP), P()),
        out_specs=P(PAIR, GRP, None),
        check_vma=False,
    )
```

time: 516 us -> 153 us (0.30)
  waiting for transfers between devices: 428 us -> 63.5 us
  starting transfers between devices: 5.99 us -> 52.6 us
  local copies, waits for them, and re-layouts: 43.2 us -> 17.4 us
  between operations: 14.1 us -> 0.34 us
  matrix products: 19.6 us -> 12 us
    all_gather x1 -> x0, waiting for transfers between devices: 234 us -> none  [on_device(): piece = lax.all_gather(integrals, 'grp', axis=1, tiled=True)]
    unnamed x3 -> x0, waiting for transfers between devices: 187 us -> none
    ppermute x0 -> x27, waiting for transfers between devices: none -> 63.5 us  [the longest x13 40.4 us: swap(): return lax.ppermute(x, axes, [(i, i ^ bits) for i in range(n)])]
    ppermute x0 -> x27, starting transfers between devices: none -> 52.6 us  [the longest x14 38 us: along_z(): return lax.ppermute(x, 'z', [(i, (i + d) % NZ) for i in range(NZ)])]
    unnamed x16 -> x26, local copies, waits for them, and re-layouts: 23.2 us -> 5.67 us
    reshape x2 -> x8, local copies, waits for them, and re-layouts: 12.7 us -> 4.75 us  [the longest x7 4.72 us: on_device(): flat = jnp.stack([g.reshape(2, 4, nr, depth) for g in got], axis=2)]
    dot_general x3 -> x8, matrix products: 19.6 us -> 12 us  [dot(): jnp.dot(a, b, precision=lax.Precision.HIGH, preferred_element_type=jnp.fl...]
    all_to_all x2 -> x0, local copies, waits for them, and re-layouts: 7.09 us -> none  [on_device(): lax.all_to_all(amplitudes, 'pair', split_axis=2, concat_axis=0, tiled=True)]
  transfers between devices with their start and end apart: 3 -> 27, of which waited for: 3 -> 17; matrix products, arithmetic and copies ran while one was open for 6% -> 18% of each run, Pallas kernels for 0% -> 0%
where the time goes in v1:
time: 153 us; the launch traced here: 152 us
  waiting for transfers between devices  63.5 us (42%)
  starting transfers between devices  52.6 us (34%)
  local copies, waits for them, and re-layouts  17.4 us (11%)
  matrix products  12 us (8%)
  Pallas kernels  5.11 us (3%)
    ppermute x13, waiting for transfers between devices, swap(): return lax.ppermute(x, axes, [(i, i ^ bits) for i in range(n)])  40.4 us
    ppermute x14, starting transfers between devices, along_z(): return lax.ppermute(x, 'z', [(i, (i + d) % NZ) for i in range(NZ)])  38 us
    ppermute x14, waiting for transfers between devices, along_z(): return lax.ppermute(x, 'z', [(i, (i + d) % NZ) for i in range(NZ)])  23.1 us
    ppermute x13, starting transfers between devices, swap(): return lax.ppermute(x, axes, [(i, i ^ bits) for i in range(n)])  14.6 us
    dot_general x8, matrix products, dot(): jnp.dot(a, b, precision=lax.Precision.HIGH, preferred_element_type=jnp.fl...  12 us
    unnamed x26, local copies, waits for them, and re-layouts  5.67 us
    reshape x7, local copies, waits for them, and re-layouts, on_device(): flat = jnp.stack([g.reshape(2, 4, nr, depth) for g in got], axis=2)  4.72 us
    another operation x2, local copies, waits for them, and re-layouts, on_device(): flat = jnp.stack([g.reshape(2, 4, nr, depth) for g in got], axis=2)  3.25 us
  transfers between devices with their start and end apart: 27, of which 17 were waited for; matrix products, arithmetic and copies ran while one was open for 18% of the time, Pallas kernels for 0%

profile of v1, /device:TPU:2, one launch (start us, length us, event | category | flops | bytes accessed | tf_op | source)
XLA Modules:
  0.0 152.0 jit_solution(1595104030559938107)
XLA Ops:
  0.0 2.6 %mask.1 = f32[2,4,9,512]{3,2,1,0:T(8,128)} custom-call(s32[8]{0:T(128)} %occ_ref.1, s32[8]{0:T(128)} %vir_ref.1, s32[8,8]{1,0:T(8,128)} %mask_ref.1, f32[3,3,4096]{2,1,0:T(4,128)} %a_ref.1), custom_call_target="tpu_custom_call" | custom-call | tf_op jit(solution)/shard_map/mask/pallas_call | solution.py:60
  6.7 2.9 %collective-permute-start.2 = (f32[2,9,512]{2,1,0:T(8,128)S(1)}, f32[2,9,512]{2,1,0:T(8,128)S(1)}, u32[]{:S(2)}, u32[]{:S(2)}) collective-permute-start(f32[2,9,512]{2,1,0:T(8,128)S(1)} %get-tuple-element.20), channel_id=1, source_target_pairs={{0,64},{32,96},{64,0},{96,32},{1,65},{33,97},{65,1},{97,33},{2,66}... | collective-permute-start | bytes 110600 | tf_op jit(solution)/shard_map/exchange_amplitudes/ppermute | solution.py:19
  9.9 3.3 %collective-permute-done.2 = f32[2,9,512]{2,1,0:T(8,128)S(1)} collective-permute-done((f32[2,9,512]{2,1,0:T(8,128)S(1)}, f32[2,9,512]{2,1,0:T(8,128)S(1)}, u32[]{:S(2)}, u32[]{:S(2)}) %collective-permute-start.2) | collective-permute-done | bytes 36896 | tf_op jit(solution)/shard_map/exchange_amplitudes/ppermute | solution.py:19
  15.2 2.0 %collective-permute-start.4 = (f32[72,512]{1,0:T(8,128)S(1)}, f32[72,512]{1,0:T(8,128)S(1)}, u32[]{:S(2)}, u32[]{:S(2)}) collective-permute-start(f32[72,512]{1,0:T(8,128)S(1)} %reshape.60), channel_id=1, source_target_pairs={{0,2},{2,4},{4,6},{6,8},{8,10},{10,12},{12,14},{14,0},{1,3},{3,5},... | collective-permute-start | bytes 442376 | tf_op jit(solution)/shard_map/gather_amplitudes/ppermute | solution.py:23
  17.7 2.2 %collective-permute-start.16 = (f32[256,1280]{1,0:T(8,128)S(1)}, f32[256,1280]{1,0:T(8,128)S(1)}, u32[]{:S(2)}, u32[]{:S(2)}) collective-permute-start(f32[256,1280]{1,0:T(8,128)S(1)} %copy-done), channel_id=1, source_target_pairs={{0,129},{1,128},{128,1},{129,0},{2,131},{3,130},{130,3},{131,2},{4... | collective-permute-start | bytes 3932168 | tf_op jit(solution)/shard_map/gather_integrals/ppermute | solution.py:19
  19.9 3.3 %collective-permute-start.5 = (f32[72,512]{1,0:T(8,128)S(1)}, f32[72,512]{1,0:T(8,128)}, u32[]{:S(2)}, u32[]{:S(2)}) collective-permute-start(f32[72,512]{1,0:T(8,128)S(1)} %reshape.60), channel_id=1, source_target_pairs={{0,4},{2,6},{4,8},{6,10},{8,12},{10,14},{12,0},{14,2},{1,5},{3,7},... | collective-permute-start | bytes 442376 | tf_op jit(solution)/shard_map/gather_amplitudes/ppermute | solution.py:23
  23.2 4.0 %collective-permute-start.6 = (f32[72,512]{1,0:T(8,128)S(1)}, f32[72,512]{1,0:T(8,128)S(1)}, u32[]{:S(2)}, u32[]{:S(2)}) collective-permute-start(f32[72,512]{1,0:T(8,128)S(1)} %reshape.60), channel_id=1, source_target_pairs={{0,6},{2,8},{4,10},{6,12},{8,14},{10,0},{12,2},{14,4},{1,7},{3,9},... | collective-permute-start | bytes 442376 | tf_op jit(solution)/shard_map/gather_amplitudes/ppermute | solution.py:23
  28.6 2.4 %collective-permute-start.7 = (f32[72,512]{1,0:T(8,128)S(1)}, f32[72,512]{1,0:T(8,128)S(1)}, u32[]{:S(2)}, u32[]{:S(2)}) collective-permute-start(f32[72,512]{1,0:T(8,128)S(1)} %reshape.60), channel_id=1, source_target_pairs={{0,8},{2,10},{4,12},{6,14},{8,0},{10,2},{12,4},{14,6},{1,9},{3,11}... | collective-permute-start | bytes 442376 | tf_op jit(solution)/shard_map/gather_amplitudes/ppermute | solution.py:23
  32.6 4.1 %collective-permute-done.5 = f32[72,512]{1,0:T(8,128)} collective-permute-done((f32[72,512]{1,0:T(8,128)S(1)}, f32[72,512]{1,0:T(8,128)}, u32[]{:S(2)}, u32[]{:S(2)}) %collective-permute-start.5) | collective-permute-done | bytes 147488 | tf_op jit(solution)/shard_map/gather_amplitudes/ppermute | solution.py:23
  36.7 2.8 %collective-permute-start.8 = (f32[72,512]{1,0:T(8,128)S(1)}, f32[72,512]{1,0:T(8,128)}, u32[]{:S(2)}, u32[]{:S(2)}) collective-permute-start(f32[72,512]{1,0:T(8,128)S(1)} %reshape.60), channel_id=1, source_target_pairs={{0,10},{2,12},{4,14},{6,0},{8,2},{10,4},{12,6},{14,8},{1,11},{3,13... | collective-permute-start | bytes 442376 | tf_op jit(solution)/shard_map/gather_amplitudes/ppermute | solution.py:23
  41.2 4.4 %collective-permute-done.6 = f32[72,512]{1,0:T(8,128)S(1)} collective-permute-done((f32[72,512]{1,0:T(8,128)S(1)}, f32[72,512]{1,0:T(8,128)S(1)}, u32[]{:S(2)}, u32[]{:S(2)}) %collective-permute-start.6) | collective-permute-done | bytes 147488 | tf_op jit(solution)/shard_map/gather_amplitudes/ppermute | solution.py:23
  45.6 5.4 %collective-permute-start.9 = (f32[72,512]{1,0:T(8,128)S(1)}, f32[72,512]{1,0:T(8,128)}, u32[]{:S(2)}, u32[]{:S(2)}) collective-permute-start(f32[72,512]{1,0:T(8,128)S(1)} %reshape.60), channel_id=1, source_target_pairs={{0,12},{2,14},{4,0},{6,2},{8,4},{10,6},{12,8},{14,10},{1,13},{3,15... | collective-permute-start | bytes 442376 | tf_op jit(solution)/shard_map/gather_amplitudes/ppermute | solution.py:23
  52.5 2.1 %collective-permute-start.15 = (f32[256,1280]{1,0:T(8,128)S(1)}, f32[256,1280]{1,0:T(8,128)}, u32[]{:S(2)}, u32[]{:S(2)}) collective-permute-start(f32[256,1280]{1,0:T(8,128)S(1)} %copy-done), channel_id=1, source_target_pairs={{0,1},{1,0},{2,3},{3,2},{4,5},{5,4},{6,7},{7,6},{8,9},{9,8},{10,11... | collective-permute-start | bytes 3932168 | tf_op jit(solution)/shard_map/gather_integrals/ppermute | solution.py:19
  60.1 2.5 %copy.23 = f32[2,4,8,9,512]{4,0,3,2,1:T(2,128)S(1)} copy(f32[2,4,8,9,512]{4,3,0,1,2:T(8,128)} %copy_dynamic-update-slice_fusion) | data formatting | bytes 2359296 | tf_op jit(solution)/shard_map/gather_amplitudes/stack | solution.py:113
  64.4 2.1 %convolution_add_fusion.2 = f32[288,1280]{1,0:T(8,128)S(1)} fusion(f32[288,1280]{1,0:T(8,128)S(1)} %fusion.12, f32[256,1280]{1,0:T(8,128)} %collective-permute-done.11, f32[1,288,256]{2,0,1:T(1,128)S(1)} %get-tuple-element.6), kind=kOutput, calls=%fused_computation.3 | convolution fusion | flops 566599680 | bytes 4554752 | tf_op jit(solution)/shard_map/product/dot_general | solution.py:94
  66.6 7.6 %collective-permute-done.16 = f32[256,1280]{1,0:T(8,128)S(1)} collective-permute-done((f32[256,1280]{1,0:T(8,128)S(1)}, f32[256,1280]{1,0:T(8,128)S(1)}, u32[]{:S(2)}, u32[]{:S(2)}) %collective-permute-start.16) | collective-permute-done | bytes 1310752 | tf_op jit(solution)/shard_map/gather_integrals/ppermute | solution.py:19
  75.6 2.1 %convolution_add_fusion = f32[288,1280]{1,0:T(8,128)S(1)} fusion(f32[288,1280]{1,0:T(8,128)S(1)} %fusion.8, f32[256,1280]{1,0:T(8,128)} %collective-permute-done.15, f32[1,288,256]{2,0,1:T(1,128)S(1)} %get-tuple-element.7), kind=kOutput, calls=%fused_computation | convolution fusion | flops 566599680 | bytes 4554752 | tf_op jit(solution)/shard_map/product/dot_general | solution.py:94
  78.7 2.2 %fusion.1 = f32[288,1280]{1,0:T(8,128)S(1)} fusion(f32[288,1280]{1,0:T(8,128)S(1)} %collective-permute-done.12, f32[288,1280]{1,0:T(8,128)S(1)} %fusion.18, f32[256,1280]{1,0:T(8,128)} %collective-permute-done.11, f32[1,288,256]{2,0,1:T(1,128)S(1)} %get-tuple-element.5), kind=kOutput, calls=%fused_computation.5 | convolution fusion | flops 566968320 | bytes 6029312 | tf_op jit(solution)/shard_map/product/dot_general | solution.py:94
  82.3 2.2 %fusion = f32[288,1280]{1,0:T(8,128)S(1)} fusion(f32[288,1280]{1,0:T(8,128)S(1)} %collective-permute-done.17, f32[288,1280]{1,0:T(8,128)S(1)} %fusion.14, f32[256,1280]{1,0:T(8,128)} %collective-permute-done.15, f32[1,288,256]{2,0,1:T(1,128)S(1)} %get-tuple-element.8), kind=kOutput, calls=%fused_computation.2 | convolution fusion | flops 566968320 | bytes 6029312 | tf_op jit(solution)/shard_map/product/dot_general | solution.py:94
  86.1 13.8 %collective-permute-done.13 = f32[2,72,1280]{2,1,0:T(8,128)S(1)} collective-permute-done((f32[2,72,1280]{2,1,0:T(8,128)S(1)}, f32[2,72,1280]{2,1,0:T(8,128)S(1)}, u32[]{:S(2)}, u32[]{:S(2)}) %collective-permute-start.13) | collective-permute-done | bytes 737312 | tf_op jit(solution)/shard_map/sum_y/ppermute | solution.py:19
  101.9 3.2 %collective-permute-done.18 = f32[2,72,1280]{2,1,0:T(8,128)S(1)} collective-permute-done((f32[2,72,1280]{2,1,0:T(8,128)S(1)}, f32[2,72,1280]{2,1,0:T(8,128)S(1)}, u32[]{:S(2)}, u32[]{:S(2)}) %collective-permute-start.18) | collective-permute-done | bytes 737312 | tf_op jit(solution)/shard_map/sum_y/ppermute | solution.py:19
  106.0 6.4 %collective-permute-done.14 = f32[72,1280]{1,0:T(8,128)S(1)} collective-permute-done((f32[72,1280]{1,0:T(8,128)S(1)}, f32[72,1280]{1,0:T(8,128)S(1)}, u32[]{:S(2)}, u32[]{:S(2)}) %collective-permute-start.14) | collective-permute-done | bytes 368672 | tf_op jit(solution)/shard_map/sum_y/ppermute | solution.py:19
  112.4 2.3 %collective-permute-done.19 = f32[72,1280]{1,0:T(8,128)S(1)} collective-permute-done((f32[72,1280]{1,0:T(8,128)S(1)}, f32[72,1280]{1,0:T(8,128)S(1)}, u32[]{:S(2)}, u32[]{:S(2)}) %collective-permute-start.19) | collective-permute-done | bytes 368672 | tf_op jit(solution)/shard_map/sum_y/ppermute | solution.py:19
  115.0 7.5 %collective-permute-start.20 = (f32[3,3,2560]{2,1,0:T(4,128)S(1)}, f32[3,3,2560]{2,1,0:T(4,128)S(1)}, u32[]{:S(2)}, u32[]{:S(2)}) collective-permute-start(f32[3,3,2560]{2,1,0:T(4,128)S(1)} %squeeze.89), channel_id=1, source_target_pairs={{0,14},{2,0},{4,2},{6,4},{8,6},{10,8},{12,10},{14,12},{1,15},{3,1}... | collective-permute-start | bytes 276488 | tf_op jit(solution)/shard_map/to_owner/ppermute | solution.py:23
  122.6 2.7 %collective-permute-start.22 = (f32[3,3,2560]{2,1,0:T(4,128)S(1)}, f32[3,3,2560]{2,1,0:T(4,128)S(1)}, u32[]{:S(2)}, u32[]{:S(2)}) collective-permute-start(f32[3,3,2560]{2,1,0:T(4,128)S(1)} %squeeze.91), channel_id=1, source_target_pairs={{0,10},{2,12},{4,14},{6,0},{8,2},{10,4},{12,6},{14,8},{1,11},{3,13... | collective-permute-start | bytes 276488 | tf_op jit(solution)/shard_map/to_owner/ppermute | solution.py:23
  125.3 3.7 %collective-permute-start.23 = (f32[3,3,2560]{2,1,0:T(4,128)S(1)}, f32[3,3,2560]{2,1,0:T(4,128)S(1)}, u32[]{:S(2)}, u32[]{:S(2)}) collective-permute-start(f32[3,3,2560]{2,1,0:T(4,128)S(1)} %squeeze.92), channel_id=1, source_target_pairs={{0,8},{2,10},{4,12},{6,14},{8,0},{10,2},{12,4},{14,6},{1,9},{3,11}... | collective-permute-start | bytes 276488 | tf_op jit(solution)/shard_map/to_owner/ppermute | solution.py:23
  129.3 4.1 %collective-permute-start.25 = (f32[3,3,2560]{2,1,0:T(4,128)S(1)}, f32[3,3,2560]{2,1,0:T(4,128)S(1)}, u32[]{:S(2)}, u32[]{:S(2)}) collective-permute-start(f32[3,3,2560]{2,1,0:T(4,128)S(1)} %squeeze.94), channel_id=1, source_target_pairs={{0,4},{2,6},{4,8},{6,10},{8,12},{10,14},{12,0},{14,2},{1,5},{3,7},... | collective-permute-start | bytes 276488 | tf_op jit(solution)/shard_map/to_owner/ppermute | solution.py:23
  133.4 2.0 %collective-permute-done.21.refs_2_ = f32[3,3,2560]{2,1,0:T(4,128)S(1)} collective-permute-done((f32[3,3,2560]{2,1,0:T(4,128)S(1)}, f32[3,3,2560]{2,1,0:T(4,128)S(1)}, u32[]{:S(2)}, u32[]{:S(2)}) %collective-permute-start.21) | collective-permute-done | bytes 92192 | tf_op jit(solution)/shard_map/to_owner/ppermute | solution.py:23
  136.8 5.2 %collective-permute-done.22.refs_3_ = f32[3,3,2560]{2,1,0:T(4,128)S(1)} collective-permute-done((f32[3,3,2560]{2,1,0:T(4,128)S(1)}, f32[3,3,2560]{2,1,0:T(4,128)S(1)}, u32[]{:S(2)}, u32[]{:S(2)}) %collective-permute-start.22) | collective-permute-done | bytes 92192 | tf_op jit(solution)/shard_map/to_owner/ppermute | solution.py:23
  142.0 3.0 %collective-permute-done.24.refs_5_ = f32[3,3,2560]{2,1,0:T(4,128)S(1)} collective-permute-done((f32[3,3,2560]{2,1,0:T(4,128)S(1)}, f32[3,3,2560]{2,1,0:T(4,128)S(1)}, u32[]{:S(2)}, u32[]{:S(2)}) %collective-permute-start.24) | collective-permute-done | bytes 92192 | tf_op jit(solution)/shard_map/to_owner/ppermute | solution.py:23
  145.1 3.4 %collective-permute-done.25.refs_6_ = f32[3,3,2560]{2,1,0:T(4,128)S(1)} collective-permute-done((f32[3,3,2560]{2,1,0:T(4,128)S(1)}, f32[3,3,2560]{2,1,0:T(4,128)S(1)}, u32[]{:S(2)}, u32[]{:S(2)}) %collective-permute-start.25) | collective-permute-done | bytes 92192 | tf_op jit(solution)/shard_map/to_owner/ppermute | solution.py:23
  149.5 2.5 %scale.1 = f32[3,3,20480]{2,1,0:T(4,128)} custom-call(f32[3,3,2560]{2,1,0:T(4,128)} %squeeze.88.refs_0_, f32[3,3,2560]{2,1,0:T(4,128)} %copy-done.2, f32[3,3,2560]{2,1,0:T(4,128)} %copy-done.3, f32[3,3,2560]{2,1,0:T(4,128)} %copy-done.4, f32[3,3,2560]{2,1,0:T(4,128)} %copy-done.5, f32[3,3,2560]{2,1,0:T(4,128)} %copy-done.6, f32[3,3,2560]{2,1,0:T(4,128)} %copy-done.7, ...), custom_call_target="tpu_custom_call" | custom-call | tf_op jit(solution)/shard_map/scale/pallas_call | solution.py:85
  (90 shorter events, 31.6 us)
Async XLA Ops:
  0.0 17.2 %copy-start = (f32[256,1280]{1,0:T(8,128)S(1)}, f32[256,1280]{1,0:T(8,128)}, u32[]{:S(2)}) copy-start(f32[256,1280]{1,0:T(8,128)} %param.8) | copy-start | bytes 3932164
  3.6 1.4 collective-permute-start
  5.1 4.8 %collective-permute-start.1 = (f32[2,9,512]{2,1,0:T(8,128)S(1)}, f32[2,9,512]{2,1,0:T(8,128)S(1)}, u32[]{:S(2)}, u32[]{:S(2)}) collective-permute-start(f32[2,9,512]{2,1,0:T(8,128)S(1)} %get-tuple-element.18), channel_id=1, source_target_pairs={{0,32},{32,0},{64,96},{96,64},{1,33},{33,1},{65,97},{97,65},{2,34}... | collective-permute-start | bytes 110600 | tf_op jit(solution)/shard_map/exchange_amplitudes/ppermute | solution.py:19
  6.7 6.4 %collective-permute-start.2 = (f32[2,9,512]{2,1,0:T(8,128)S(1)}, f32[2,9,512]{2,1,0:T(8,128)S(1)}, u32[]{:S(2)}, u32[]{:S(2)}) collective-permute-start(f32[2,9,512]{2,1,0:T(8,128)S(1)} %get-tuple-element.20), channel_id=1, source_target_pairs={{0,64},{32,96},{64,0},{96,32},{1,65},{33,97},{65,1},{97,33},{2,66}... | collective-permute-start | bytes 110600 | tf_op jit(solution)/shard_map/exchange_amplitudes/ppermute | solution.py:19
  9.6 5.5 %collective-permute-start.3 = (f32[2,9,512]{2,1,0:T(8,128)S(1)}, f32[2,9,512]{2,1,0:T(8,128)S(1)}, u32[]{:S(2)}, u32[]{:S(2)}) collective-permute-start(f32[2,9,512]{2,1,0:T(8,128)S(1)} %get-tuple-element.19), channel_id=1, source_target_pairs={{0,96},{32,64},{64,32},{96,0},{1,97},{33,65},{65,33},{97,1},{2,98}... | collective-permute-start | bytes 110600 | tf_op jit(solution)/shard_map/exchange_amplitudes/ppermute | solution.py:19
  15.2 12.7 %collective-permute-start.4 = (f32[72,512]{1,0:T(8,128)S(1)}, f32[72,512]{1,0:T(8,128)S(1)}, u32[]{:S(2)}, u32[]{:S(2)}) collective-permute-start(f32[72,512]{1,0:T(8,128)S(1)} %reshape.60), channel_id=1, source_target_pairs={{0,2},{2,4},{4,6},{6,8},{8,10},{10,12},{12,14},{14,0},{1,3},{3,5},... | collective-permute-start | bytes 442376 | tf_op jit(solution)/shard_map/gather_amplitudes/ppermute | solution.py:23
  17.2 47.2 %collective-permute-start.11 = (f32[256,1280]{1,0:T(8,128)S(1)}, f32[256,1280]{1,0:T(8,128)}, u32[]{:S(2)}, u32[]{:S(2)}) collective-permute-start(f32[256,1280]{1,0:T(8,128)S(1)} %copy-done), channel_id=1, source_target_pairs={{0,128},{128,0},{1,129},{129,1},{2,130},{130,2},{3,131},{131,3},{4... | collective-permute-start | bytes 3932168 | tf_op jit(solution)/shard_map/gather_integrals/ppermute | solution.py:19
  17.7 56.5 %collective-permute-start.16 = (f32[256,1280]{1,0:T(8,128)S(1)}, f32[256,1280]{1,0:T(8,128)S(1)}, u32[]{:S(2)}, u32[]{:S(2)}) collective-permute-start(f32[256,1280]{1,0:T(8,128)S(1)} %copy-done), channel_id=1, source_target_pairs={{0,129},{1,128},{128,1},{129,0},{2,131},{3,130},{130,3},{131,2},{4... | collective-permute-start | bytes 3932168 | tf_op jit(solution)/shard_map/gather_integrals/ppermute | solution.py:19
  19.9 16.8 %collective-permute-start.5 = (f32[72,512]{1,0:T(8,128)S(1)}, f32[72,512]{1,0:T(8,128)}, u32[]{:S(2)}, u32[]{:S(2)}) collective-permute-start(f32[72,512]{1,0:T(8,128)S(1)} %reshape.60), channel_id=1, source_target_pairs={{0,4},{2,6},{4,8},{6,10},{8,12},{10,14},{12,0},{14,2},{1,5},{3,7},... | collective-permute-start | bytes 442376 | tf_op jit(solution)/shard_map/gather_amplitudes/ppermute | solution.py:23
  23.2 22.4 %collective-permute-start.6 = (f32[72,512]{1,0:T(8,128)S(1)}, f32[72,512]{1,0:T(8,128)S(1)}, u32[]{:S(2)}, u32[]{:S(2)}) collective-permute-start(f32[72,512]{1,0:T(8,128)S(1)} %reshape.60), channel_id=1, source_target_pairs={{0,6},{2,8},{4,10},{6,12},{8,14},{10,0},{12,2},{14,4},{1,7},{3,9},... | collective-permute-start | bytes 442376 | tf_op jit(solution)/shard_map/gather_amplitudes/ppermute | solution.py:23
  28.6 23.1 %collective-permute-start.7 = (f32[72,512]{1,0:T(8,128)S(1)}, f32[72,512]{1,0:T(8,128)S(1)}, u32[]{:S(2)}, u32[]{:S(2)}) collective-permute-start(f32[72,512]{1,0:T(8,128)S(1)} %reshape.60), channel_id=1, source_target_pairs={{0,8},{2,10},{4,12},{6,14},{8,0},{10,2},{12,4},{14,6},{1,9},{3,11}... | collective-permute-start | bytes 442376 | tf_op jit(solution)/shard_map/gather_amplitudes/ppermute | solution.py:23
  36.7 15.7 %collective-permute-start.8 = (f32[72,512]{1,0:T(8,128)S(1)}, f32[72,512]{1,0:T(8,128)}, u32[]{:S(2)}, u32[]{:S(2)}) collective-permute-start(f32[72,512]{1,0:T(8,128)S(1)} %reshape.60), channel_id=1, source_target_pairs={{0,10},{2,12},{4,14},{6,0},{8,2},{10,4},{12,6},{14,8},{1,11},{3,13... | collective-permute-start | bytes 442376 | tf_op jit(solution)/shard_map/gather_amplitudes/ppermute | solution.py:23
  45.6 9.9 %collective-permute-start.9 = (f32[72,512]{1,0:T(8,128)S(1)}, f32[72,512]{1,0:T(8,128)}, u32[]{:S(2)}, u32[]{:S(2)}) collective-permute-start(f32[72,512]{1,0:T(8,128)S(1)} %reshape.60), channel_id=1, source_target_pairs={{0,12},{2,14},{4,0},{6,2},{8,4},{10,6},{12,8},{14,10},{1,13},{3,15... | collective-permute-start | bytes 442376 | tf_op jit(solution)/shard_map/gather_amplitudes/ppermute | solution.py:23
  51.7 5.3 %collective-permute-start.10 = (f32[72,512]{1,0:T(8,128)S(1)}, f32[72,512]{1,0:T(8,128)}, u32[]{:S(2)}, u32[]{:S(2)}) collective-permute-start(f32[72,512]{1,0:T(8,128)S(1)} %reshape.60), channel_id=1, source_target_pairs={{0,14},{2,0},{4,2},{6,4},{8,6},{10,8},{12,10},{14,12},{1,15},{3,1}... | collective-permute-start | bytes 442376 | tf_op jit(solution)/shard_map/gather_amplitudes/ppermute | solution.py:23
  52.5 23.1 %collective-permute-start.15 = (f32[256,1280]{1,0:T(8,128)S(1)}, f32[256,1280]{1,0:T(8,128)}, u32[]{:S(2)}, u32[]{:S(2)}) collective-permute-start(f32[256,1280]{1,0:T(8,128)S(1)} %copy-done), channel_id=1, source_target_pairs={{0,1},{1,0},{2,3},{3,2},{4,5},{5,4},{6,7},{7,6},{8,9},{9,8},{10,11... | collective-permute-start | bytes 3932168 | tf_op jit(solution)/shard_map/gather_integrals/ppermute | solution.py:19
  66.5 12.1 %collective-permute-start.12 = (f32[288,1280]{1,0:T(8,128)S(1)}, f32[288,1280]{1,0:T(8,128)S(1)}, u32[]{:S(2)}, u32[]{:S(2)}) collective-permute-start(f32[288,1280]{1,0:T(8,128)S(1)} %convolution_add_fusion.2), channel_id=1, source_target_pairs={{0,16},{16,0},{1,17},{17,1},{2,18},{18,2},{3,19},{19,3},{4,20},{20... | collective-permute-start | bytes 4423688 | tf_op jit(solution)/shard_map/sum_core/ppermute | solution.py:19
  77.8 4.5 %collective-permute-start.17 = (f32[288,1280]{1,0:T(8,128)S(1)}, f32[288,1280]{1,0:T(8,128)S(1)}, u32[]{:S(2)}, u32[]{:S(2)}) collective-permute-start(f32[288,1280]{1,0:T(8,128)S(1)} %convolution_add_fusion), channel_id=1, source_target_pairs={{0,16},{16,0},{1,17},{17,1},{2,18},{18,2},{3,19},{19,3},{4,20},{20... | collective-permute-start | bytes 4423688 | tf_op jit(solution)/shard_map/sum_core/ppermute | solution.py:19
  81.0 19.0 %collective-permute-start.13 = (f32[2,72,1280]{2,1,0:T(8,128)S(1)}, f32[2,72,1280]{2,1,0:T(8,128)S(1)}, u32[]{:S(2)}, u32[]{:S(2)}) collective-permute-start(f32[2,72,1280]{2,1,0:T(8,128)S(1)} %bitcast.78), channel_id=1, source_target_pairs={{0,32},{32,0},{64,96},{96,64},{1,33},{33,1},{65,97},{97,65},{2,34}... | collective-permute-start | bytes 2211848 | tf_op jit(solution)/shard_map/sum_y/ppermute | solution.py:19
  84.5 20.6 %collective-permute-start.18 = (f32[2,72,1280]{2,1,0:T(8,128)S(1)}, f32[2,72,1280]{2,1,0:T(8,128)S(1)}, u32[]{:S(2)}, u32[]{:S(2)}) collective-permute-start(f32[2,72,1280]{2,1,0:T(8,128)S(1)} %bitcast.79), channel_id=1, source_target_pairs={{0,96},{32,64},{64,32},{96,0},{1,97},{33,65},{65,33},{97,1},{2,98}... | collective-permute-start | bytes 2211848 | tf_op jit(solution)/shard_map/sum_y/ppermute | solution.py:19
  100.0 12.3 %collective-permute-start.14 = (f32[72,1280]{1,0:T(8,128)S(1)}, f32[72,1280]{1,0:T(8,128)S(1)}, u32[]{:S(2)}, u32[]{:S(2)}) collective-permute-start(f32[72,1280]{1,0:T(8,128)S(1)} %fusion.5), channel_id=1, source_target_pairs={{0,96},{32,64},{64,32},{96,0},{1,97},{33,65},{65,33},{97,1},{2,98}... | collective-permute-start | bytes 1105928 | tf_op jit(solution)/shard_map/sum_y/ppermute | solution.py:19
  105.2 9.5 %collective-permute-start.19 = (f32[72,1280]{1,0:T(8,128)S(1)}, f32[72,1280]{1,0:T(8,128)S(1)}, u32[]{:S(2)}, u32[]{:S(2)}) collective-permute-start(f32[72,1280]{1,0:T(8,128)S(1)} %fusion.2), channel_id=1, source_target_pairs={{0,32},{32,0},{64,96},{96,64},{1,33},{33,1},{65,97},{97,65},{2,34}... | collective-permute-start | bytes 1105928 | tf_op jit(solution)/shard_map/sum_y/ppermute | solution.py:19
  114.9 20.6 %copy-start.9 = (f32[3,3]{1,0:T(4,128)S(1)}, f32[3,3]{1,0:T(4,128)}, u32[]{:S(2)}) copy-start(f32[3,3]{1,0:T(4,128)} %param.12) | copy-start | bytes 112
  115.0 14.3 %collective-permute-start.20 = (f32[3,3,2560]{2,1,0:T(4,128)S(1)}, f32[3,3,2560]{2,1,0:T(4,128)S(1)}, u32[]{:S(2)}, u32[]{:S(2)}) collective-permute-start(f32[3,3,2560]{2,1,0:T(4,128)S(1)} %squeeze.89), channel_id=1, source_target_pairs={{0,14},{2,0},{4,2},{6,4},{8,6},{10,8},{12,10},{14,12},{1,15},{3,1}... | collective-permute-start | bytes 276488 | tf_op jit(solution)/shard_map/to_owner/ppermute | solution.py:23
  122.5 13.0 %collective-permute-start.21 = (f32[3,3,2560]{2,1,0:T(4,128)S(1)}, f32[3,3,2560]{2,1,0:T(4,128)S(1)}, u32[]{:S(2)}, u32[]{:S(2)}) collective-permute-start(f32[3,3,2560]{2,1,0:T(4,128)S(1)} %squeeze.90), channel_id=1, source_target_pairs={{0,12},{2,14},{4,0},{6,2},{8,4},{10,6},{12,8},{14,10},{1,13},{3,15... | collective-permute-start | bytes 276488 | tf_op jit(solution)/shard_map/to_owner/ppermute | solution.py:23
  122.6 19.4 %collective-permute-start.22 = (f32[3,3,2560]{2,1,0:T(4,128)S(1)}, f32[3,3,2560]{2,1,0:T(4,128)S(1)}, u32[]{:S(2)}, u32[]{:S(2)}) collective-permute-start(f32[3,3,2560]{2,1,0:T(4,128)S(1)} %squeeze.91), channel_id=1, source_target_pairs={{0,10},{2,12},{4,14},{6,0},{8,2},{10,4},{12,6},{14,8},{1,11},{3,13... | collective-permute-start | bytes 276488 | tf_op jit(solution)/shard_map/to_owner/ppermute | solution.py:23
  125.3 16.7 %collective-permute-start.23 = (f32[3,3,2560]{2,1,0:T(4,128)S(1)}, f32[3,3,2560]{2,1,0:T(4,128)S(1)}, u32[]{:S(2)}, u32[]{:S(2)}) collective-permute-start(f32[3,3,2560]{2,1,0:T(4,128)S(1)} %squeeze.92), channel_id=1, source_target_pairs={{0,8},{2,10},{4,12},{6,14},{8,0},{10,2},{12,4},{14,6},{1,9},{3,11}... | collective-permute-start | bytes 276488 | tf_op jit(solution)/shard_map/to_owner/ppermute | solution.py:23
  129.1 16.0 %collective-permute-start.24 = (f32[3,3,2560]{2,1,0:T(4,128)S(1)}, f32[3,3,2560]{2,1,0:T(4,128)S(1)}, u32[]{:S(2)}, u32[]{:S(2)}) collective-permute-start(f32[3,3,2560]{2,1,0:T(4,128)S(1)} %squeeze.93), channel_id=1, source_target_pairs={{0,6},{2,8},{4,10},{6,12},{8,14},{10,0},{12,2},{14,4},{1,7},{3,9},... | collective-permute-start | bytes 276488 | tf_op jit(solution)/shard_map/to_owner/ppermute | solution.py:23
  129.3 19.6 %copy-start.2 = (f32[3,3,2560]{2,1,0:T(4,128)}, f32[3,3,2560]{2,1,0:T(4,128)S(1)}, u32[]{:S(2)}) copy-start(f32[3,3,2560]{2,1,0:T(4,128)S(1)} %collective-permute-done.20.refs_1_) | copy-start | bytes 276484
  129.3 19.2 %collective-permute-start.25 = (f32[3,3,2560]{2,1,0:T(4,128)S(1)}, f32[3,3,2560]{2,1,0:T(4,128)S(1)}, u32[]{:S(2)}, u32[]{:S(2)}) collective-permute-start(f32[3,3,2560]{2,1,0:T(4,128)S(1)} %squeeze.94), channel_id=1, source_target_pairs={{0,4},{2,6},{4,8},{6,10},{8,12},{10,14},{12,0},{14,2},{1,5},{3,7},... | collective-permute-start | bytes 276488 | tf_op jit(solution)/shard_map/to_owner/ppermute | solution.py:23
  135.5 13.4 %copy-start.3 = (f32[3,3,2560]{2,1,0:T(4,128)}, f32[3,3,2560]{2,1,0:T(4,128)S(1)}, u32[]{:S(2)}) copy-start(f32[3,3,2560]{2,1,0:T(4,128)S(1)} %collective-permute-done.21.refs_2_) | copy-start | bytes 276484
  135.5 13.4 %collective-permute-start.26 = (f32[3,3,2560]{2,1,0:T(4,128)S(1)}, f32[3,3,2560]{2,1,0:T(4,128)S(1)}, u32[]{:S(2)}, u32[]{:S(2)}) collective-permute-start(f32[3,3,2560]{2,1,0:T(4,128)S(1)} %squeeze.95), channel_id=1, source_target_pairs={{0,2},{2,4},{4,6},{6,8},{8,10},{10,12},{12,14},{14,0},{1,3},{3,5},... | collective-permute-start | bytes 276488 | tf_op jit(solution)/shard_map/to_owner/ppermute | solution.py:23
  142.0 6.9 %copy-start.5 = (f32[3,3,2560]{2,1,0:T(4,128)}, f32[3,3,2560]{2,1,0:T(4,128)S(1)}, u32[]{:S(2)}) copy-start(f32[3,3,2560]{2,1,0:T(4,128)S(1)} %collective-permute-done.23.refs_4_) | copy-start | bytes 276484
  (5 other events, 12.7 us)

commit v2 on v1

v2 whole, which is shorter than its diff:
```python
import jax
import jax.numpy as jnp
from jax import lax
from jax.experimental import pallas as pl
from jax.experimental.pallas import tpu as pltpu
from jax.sharding import Mesh, PartitionSpec as P

AXES = ("xl", "y", "core", "z", "xh")
SIZES = (2, 4, 2, 8, 2)
PAIR, GRP = ("xl", "y", "core"), ("z", "xh")
NZ = 8
CHEAP = pl.CostEstimate(flops=1000, bytes_accessed=1000, transcendentals=0)
VMEM = pl.BlockSpec(memory_space=pltpu.VMEM)
ANY = pl.BlockSpec(memory_space=pl.ANY)


def call(kernel, out_shape, operands, after=(), scratch=(), mib=8):
    several = isinstance(out_shape, list)

    def body(*refs):
        kernel(*refs[: len(operands)], *refs[len(operands) + len(after) :])

    return pl.pallas_call(
        body,
        out_shape=out_shape,
        in_specs=[VMEM] * len(operands) + [ANY] * len(after),
        out_specs=[VMEM] * len(out_shape) if several else VMEM,
        scratch_shapes=list(scratch),
        cost_estimate=CHEAP,
        compiler_params=pltpu.CompilerParams(vmem_limit_bytes=mib * 2**20),
        name=kernel.__name__,
    )(*operands, *after)


def f32(*shape):
    return jax.ShapeDtypeStruct(shape, jnp.float32)


def swap(x, axes, bits):
    names = axes if isinstance(axes, tuple) else (axes,)
    n = 1
    for a in names:
        n *= SIZES[AXES.index(a)]
    return lax.ppermute(x, axes, [(i, i ^ bits) for i in range(n)])


def along_z(x, d):
    return lax.ppermute(x, "z", [(i, (i + d) % NZ) for i in range(NZ)])


def mask_kernel(occ_ref, vir_ref, mask_ref, a_ref, near_ref, far_ref, held):
    xl, y, core = lax.axis_index("xl"), lax.axis_index("y"), lax.axis_index("core")
    z, xh = lax.axis_index("z"), lax.axis_index("xh")
    no, ni, width = a_ref.shape
    blocks = vir_ref.shape[0]
    part = width // 16
    col = lax.broadcasted_iota(jnp.int32, (1, width), 1)
    block = jnp.full((1, width), -1, jnp.int32)
    for s in range(blocks):
        block = block + (col >= vir_ref[s]).astype(jnp.int32)
    for oo in range(no):
        for ii in range(ni):
            o = ((xl * 4 + y) * 2 + core) * no + oo
            row = o * (ni * 16) + (z * 2 + xh) * ni + ii
            row_block = jnp.int32(-1)
            for s in range(occ_ref.shape[0]):
                row_block = row_block + (row >= occ_ref[s]).astype(jnp.int32)
            keep = jnp.zeros((1, width), jnp.float32)
            for v in range(blocks):
                keep = jnp.where(block == v, mask_ref[row_block, v].astype(jnp.float32), keep)
            held[oo * ni + ii : oo * ni + ii + 1, :] = a_ref[oo, ii : ii + 1, :] * keep
    for e in range(4):
        for dc in range(2):
            for dx in range(2):
                p = ((xl ^ dx) * 4 + (y ^ e)) * 2 + (core ^ dc)
                (near_ref, far_ref)[dc][e, :, dx * part : (dx + 1) * part] = held[
                    :, pl.ds(pl.multiple_of(p * part, part), part)
                ]


def mask_rows(amplitudes, occ_start, vir_start, block_mask):
    no, ni, width = amplitudes.shape
    smem = pl.BlockSpec(memory_space=pltpu.SMEM)
    half = jax.ShapeDtypeStruct((4, no * ni, width // 8), jnp.float32)
    return pl.pallas_call(
        mask_kernel,
        out_shape=[half, half],
        in_specs=[smem, smem, smem, VMEM],
        out_specs=[VMEM, VMEM],
        scratch_shapes=[pltpu.VMEM((no * ni, width), jnp.float32)],
        cost_estimate=CHEAP,
        compiler_params=pltpu.CompilerParams(vmem_limit_bytes=8 * 2**20),
    )(occ_start, vir_start, block_mask, amplitudes)


def by_row_kernel(near_ref, far_ref, *outs):
    for e in range(4):
        outs[e][0] = near_ref[e]
        outs[e][1] = far_ref[e]


def by_row(near, far):
    return call(by_row_kernel, [f32(2, *near.shape[1:])] * 4, (near, far))


def line_up_kernel(*refs):
    rows, out_ref = refs[:4], refs[-1]
    nr = rows[0].shape[1]
    for dc in range(2):
        for e in range(4):
            at = (dc * 4 + e) * nr
            out_ref[at : at + nr, :] = rows[e][dc]


def line_up(rows):
    _, nr, depth = rows[0].shape
    return call(line_up_kernel, f32(8 * nr, depth), rows)


def pair_up_kernel(a, b, c, d, left, right):
    n = a.shape[0]
    left[:n], left[n:] = a[...], b[...]
    right[:n], right[n:] = c[...], d[...]


def pair_up(mine, down1, up1, across):
    n, depth = mine.shape
    return call(pair_up_kernel, [f32(2 * n, depth)] * 2, (mine, down1, mine, up1), (across,))


def pass_on_kernel(two, up1, six, down1, up, down):
    up[0], up[1] = two[...], up1[1]
    down[0], down[1] = six[...], down1[1]


def pass_on(two, up1, six, down1, across):
    return call(pass_on_kernel, [f32(*up1.shape)] * 2, (two, up1, six, down1), (across,))


def order_kernel(*refs):
    own, down1, up1, across, down, up = refs[:6]
    highs, lows, held = (refs[6], refs[8]), (refs[7], refs[9]), refs[10]
    n = own.shape[0]
    nr = n // 8
    source = [(own, 0), (down1, 0), (down, 0), (down, n), (across, 0), (up, n), (up, 0), (up1, 0)]
    for dc in range(2):
        for e in range(4):
            for d, (ref, base) in enumerate(source):
                at = (e * NZ + d) * nr
                where = base + (dc * 4 + e) * nr
                held[at : at + nr, :] = ref[where : where + nr, :]
        value = held[...]
        high = value.astype(jnp.bfloat16)
        highs[dc][...] = high
        lows[dc][...] = (value - high.astype(jnp.float32)).astype(jnp.bfloat16)


def order_rows(*blocks):
    n, depth = blocks[0].shape
    part = jax.ShapeDtypeStruct((4 * n, depth), jnp.bfloat16)
    return call(order_kernel, [part] * 4, blocks, scratch=[pltpu.VMEM((4 * n, depth), jnp.float32)])


def halve_kernel(a, b, first, second):
    n = first.shape[0]
    first[...] = a[:n, :]
    second[...] = b[n:, :]


def halve(a, b, after):
    depth, width = a.shape
    return call(halve_kernel, [f32(depth // 2, width)] * 2, (a, b), after)


def three_passes(high_ref, low_ref, b_refs, cols, b_high, b_low):
    at = 0
    for ref in b_refs:
        value = ref[:, cols]
        high = value.astype(jnp.bfloat16)
        b_high[at : at + ref.shape[0], :] = high
        b_low[at : at + ref.shape[0], :] = (value - high.astype(jnp.float32)).astype(jnp.bfloat16)
        at += ref.shape[0]
    dot = lambda a, b: jnp.dot(a, b, preferred_element_type=jnp.float32)
    small = dot(high_ref[...], b_low[...]) + dot(low_ref[...], b_high[...])
    return small + dot(high_ref[...], b_high[...])


def theirs_kernel(high_ref, low_ref, *refs):
    b_refs, (out_ref, b_high, b_low) = refs[:-3], refs[-3:]
    width = b_high.shape[1]
    for s in range(2):
        cols = slice(s * width, (s + 1) * width)
        out_ref[:, cols] = three_passes(high_ref, low_ref, b_refs, cols, b_high, b_low)


def ours_kernel(high_ref, low_ref, *refs):
    b_refs, other_ref, outs, (b_high, b_low) = refs[:-7], refs[-7], refs[-6:-2], refs[-2:]
    width = b_high.shape[1]
    group = outs[0].shape[0] // 2
    for s in range(2):
        cols = slice(s * width, (s + 1) * width)
        value = three_passes(high_ref, low_ref, b_refs, cols, b_high, b_low) + other_ref[:, cols]
        part = [value[e * group : (e + 1) * group] for e in range(4)]
        send, keep = outs[2 * s], outs[2 * s + 1]
        gone, kept = (((1, 2), (0, 3)), ((2, 3), (0, 1)))[s]
        for k in range(2):
            send[k * group : (k + 1) * group, :] = part[gone[k]]
            keep[k * group : (k + 1) * group, :] = part[kept[k]]


def product(high, low, pieces, other=None, after=()):
    rows, depth = high.shape
    width = pieces[0].shape[1]
    scratch = [pltpu.VMEM((depth, width // 2), jnp.bfloat16)] * 2
    if other is None:
        return call(theirs_kernel, f32(rows, width), (high, low, *pieces), after, scratch, 16)
    outs = [f32(rows // 2, width // 2)] * 4
    return call(ours_kernel, outs, (high, low, *pieces, other), after, scratch, 16)


def middle_kernel(keep_a, got_a, keep_b, got_b, send_a, send_b):
    group = send_a.shape[0]
    send_a[...] = keep_a[group:, :] + got_a[group:, :]
    send_b[...] = keep_b[group:, :] + got_b[:group, :]


def middle(*args, after=()):
    n, width = args[0].shape
    return call(middle_kernel, [f32(n // 2, width)] * 2, args, after)


def finish_kernel(*refs):
    sides, outs = (refs[:3], refs[3:6]), refs[6:]
    own, up1, down1, across, two, six = outs
    group, width = sides[0][2].shape
    nr = group // NZ
    where = [own, (up1, 0), two, (up1, 1), across, (down1, 1), six, (down1, 0)]
    for s, (keep, got, last) in enumerate(sides):
        first = 0 if s == 0 else group
        value = keep[:group, :] + got[first : first + group, :] + last[...]
        for d in range(NZ):
            for j in range(width // 128):
                at = (s * (width // 128) + j) * nr
                tile = value[d * nr : (d + 1) * nr, j * 128 : (j + 1) * 128]
                if isinstance(where[d], tuple):
                    where[d][0][where[d][1], at : at + nr, :] = tile
                else:
                    where[d][at : at + nr, :] = tile


def finish(*args):
    group, width = args[2].shape
    rows = 2 * width // 128 * (group // NZ)
    one, two = f32(rows, 128), f32(2, rows, 128)
    return call(finish_kernel, [one, two, two, one, one, one], args)


def scale_kernel(*refs):
    halves, (occ_ref, vir_ref, out_ref) = (refs[:6], refs[6:12]), refs[12:]
    z, xh = lax.axis_index("z"), lax.axis_index("xh")
    no, ni, _ = out_ref.shape
    nr = no * ni
    tiles = refs[0].shape[0] // nr
    for h, (own, up1, up, across, down, down1) in enumerate(halves):
        source = [own, up1.at[0], up.at[0], up.at[1], across, down.at[1], down.at[0], down1.at[0]]
        for d, ref in enumerate(source):
            start = (lax.rem(z + d, NZ) * 2 + (xh ^ h)) * tiles
            for j in range(tiles):
                cols = pl.ds(pl.multiple_of((start + j) * 128, 128), 128)
                value = ref[j * nr : (j + 1) * nr, :] / (occ_ref[...] - vir_ref[:, cols])
                for oo in range(no):
                    out_ref[oo, :, cols] = value[oo * ni : (oo + 1) * ni]


def scale(near, far, occ_energy, vir_energy):
    no, ni = occ_energy.shape
    operands = (*near, *far, occ_energy.reshape(no * ni, 1), vir_energy[None, :])
    return call(scale_kernel, f32(no, ni, vir_energy.shape[0]), operands)


def on_device(amplitudes, integrals, occ_start, vir_start, block_mask, occ_energy, vir_energy):
    with jax.named_scope("gather_integrals"):
        xl, d = swap(integrals, "xl", 1), swap(integrals, ("xl", "xh"), 3)
    with jax.named_scope("mask"):
        near, far = mask_rows(amplitudes, occ_start, vir_start, block_mask)
    with jax.named_scope("exchange_amplitudes"):
        pair = by_row(near, swap(far, "core", 1))
        rows = [pair[0]] + [swap(pair[e], "y", e) for e in (1, 2, 3)]
        mine = line_up(rows)
    with jax.named_scope("gather_amplitudes"):
        across, down1, up1 = along_z(mine, 4), along_z(mine, 1), along_z(mine, 7)
        pairs = pair_up(mine, down1, up1, across)
        down, up = along_z(pairs[0], 2), along_z(pairs[1], 6)
        ours_high, ours_low, theirs_high, theirs_low = order_rows(mine, down1, up1, across, down, up)
    with jax.named_scope("gather_integrals"):
        first, second = halve(xl, d, after=(pairs[0],))
        first, second = swap(first, ("xl", "xh"), 3), swap(second, "xl", 1)
    pieces = ((integrals, xl), (first, second, d))
    with jax.named_scope("product"):
        theirs = [product(theirs_high, theirs_low, p) for p in pieces]
    with jax.named_scope("sum_core"):
        other = [swap(t, "core", 1) for t in theirs]
    with jax.named_scope("product"):
        sums = [product(ours_high, ours_low, pieces[0], other[0], (theirs[1],))]
        sums.append(product(ours_high, ours_low, pieces[1], other[1]))
    with jax.named_scope("sum_y"):
        got = [(swap(a, "y", 1), swap(b, "y", 3)) for a, _, b, _ in sums]
    halves = []
    for h in range(2):
        _, keep_a, _, keep_b = sums[h]
        got_a, got_b = got[h]
        with jax.named_scope("sum_y"):
            send_a, send_b = middle(keep_a, got_a, keep_b, got_b, after=(sums[1][0],) * (1 - h))
            last_a, last_b = swap(send_a, "y", 3), swap(send_b, "y", 1)
            own, up1, down1, across, two, six = finish(keep_a, got_a, last_a, keep_b, got_b, last_b)
        with jax.named_scope("to_owner"):
            across, up1, down1 = along_z(across, 4), along_z(up1, 7), along_z(down1, 1)
            up, down = pass_on(two, up1, six, down1, across)
            up, down = along_z(up, 6), along_z(down, 2)
            halves.append((own, up1, up, across, down, down1))
    with jax.named_scope("scale"):
        return scale(*halves, occ_energy, vir_energy)


def solution(mesh):
    split = Mesh(mesh.devices.reshape(SIZES), AXES)
    return jax.shard_map(
        on_device,
        mesh=split,
        in_specs=(P(PAIR, GRP, None), P(PAIR, GRP), P(), P(), P(), P(PAIR, GRP), P()),
        out_specs=P(PAIR, GRP, None),
        check_vma=False,
    )
```

time: 153 us -> 122 us (0.80)
  local copies, waits for them, and re-layouts: 17.4 us -> 3.02 us
  waiting for transfers between devices: 63.5 us -> 50.9 us
  matrix products: 12 us -> 0 us
  Pallas kernels: 5.11 us -> 10.5 us
  starting transfers between devices: 52.6 us -> 56.8 us
    ppermute x13 -> x18, waiting for transfers between devices: 40.4 us -> 22.1 us  [swap(): return lax.ppermute(x, axes, [(i, i ^ bits) for i in range(n)])]
    dot_general x8 -> x0, matrix products: 12 us -> none  [dot(): jnp.dot(a, b, precision=lax.Precision.HIGH, preferred_element_type=jnp.fl...]
    ppermute x13 -> x18, starting transfers between devices: 14.6 us -> 21.1 us  [swap(): return lax.ppermute(x, axes, [(i, i ^ bits) for i in range(n)])]
    ppermute x14 -> x15, waiting for transfers between devices: 23.1 us -> 28.8 us  [along_z(): return lax.ppermute(x, 'z', [(i, (i + d) % NZ) for i in range(NZ)])]
    pallas_call x2 -> x17, Pallas kernels: 5.11 us -> 10.5 us  [the longest x16 9.04 us: call(): pl.pallas_call(body, out_shape=out_shape, in_specs=[VMEM] * len(operands)...]
    reshape x8 -> x1, local copies, waits for them, and re-layouts: 4.75 us -> 0.08 us  [scale(): occ_energy.reshape(no * ni, 1)]
    another operation x3 -> x0, local copies, waits for them, and re-layouts: 3.26 us -> none  [the longest x2 3.25 us: on_device(): flat = jnp.stack([g.reshape(2, 4, nr, depth) for g in got], axis=2)]
    unnamed x26 -> x14, local copies, waits for them, and re-layouts: 5.67 us -> 2.94 us
  transfers between devices with their start and end apart: 27 -> 33, of which waited for: 17 -> 18; matrix products, arithmetic and copies ran while one was open for 18% -> 0% of each run, Pallas kernels for 0% -> 7%
where the time goes in v2:
time: 122 us; the launch traced here: 121 us
  starting transfers between devices  56.8 us (47%)
  waiting for transfers between devices  50.9 us (42%)
  Pallas kernels  10.5 us (9%)
  local copies, waits for them, and re-layouts  3.02 us (2%)
    ppermute x15, starting transfers between devices, along_z(): return lax.ppermute(x, 'z', [(i, (i + d) % NZ) for i in range(NZ)])  35.7 us
    ppermute x15, waiting for transfers between devices, along_z(): return lax.ppermute(x, 'z', [(i, (i + d) % NZ) for i in range(NZ)])  28.8 us
    ppermute x18, waiting for transfers between devices, swap(): return lax.ppermute(x, axes, [(i, i ^ bits) for i in range(n)])  22.1 us
    ppermute x18, starting transfers between devices, swap(): return lax.ppermute(x, axes, [(i, i ^ bits) for i in range(n)])  21.1 us
    pallas_call x16, Pallas kernels, call(): pl.pallas_call(body, out_shape=out_shape, in_specs=[VMEM] * len(operands)...  9.04 us
    unnamed x14, local copies, waits for them, and re-layouts  2.94 us
  transfers between devices with their start and end apart: 33, of which 18 were waited for; matrix products, arithmetic and copies ran while one was open for 0% of the time, Pallas kernels for 7%

profile of v2, /device:TPU:2, one launch (start us, length us, event | category | flops | bytes accessed | tf_op | source)
XLA Modules:
  0.0 121.4 jit_solution(13475359897311247301)
XLA Ops:
  0.0 2.3 %collective-permute-start.9 = (f32[256,1280]{1,0:T(8,128)}, f32[256,1280]{1,0:T(8,128)S(1)}, u32[]{:S(2)}, u32[]{:S(2)}) collective-permute-start(f32[256,1280]{1,0:T(8,128)} %refs_2_.3), channel_id=1, source_target_pairs={{0,128},{128,0},{1,129},{129,1},{2,130},{130,2},{3,131},{131,3},{4... | collective-permute-start | bytes 3932168 | tf_op jit(solution)/shard_map/gather_integrals/ppermute | solution.py:44
  8.6 1.7 %collective-permute-start.1 = (f32[2,9,512]{2,1,0:T(8,128)S(1)}, f32[2,9,512]{2,1,0:T(8,128)S(1)}, u32[]{:S(2)}, u32[]{:S(2)}) collective-permute-start(f32[2,9,512]{2,1,0:T(8,128)S(1)} %get-tuple-element.50), channel_id=1, source_target_pairs={{0,32},{32,0},{64,96},{96,64},{1,33},{33,1},{65,97},{97,65},{2,34}... | collective-permute-start | bytes 110600 | tf_op jit(solution)/shard_map/exchange_amplitudes/ppermute | solution.py:44
  10.2 2.9 %collective-permute-start.2 = (f32[2,9,512]{2,1,0:T(8,128)S(1)}, f32[2,9,512]{2,1,0:T(8,128)S(1)}, u32[]{:S(2)}, u32[]{:S(2)}) collective-permute-start(f32[2,9,512]{2,1,0:T(8,128)S(1)} %get-tuple-element.51), channel_id=1, source_target_pairs={{0,64},{32,96},{64,0},{96,32},{1,65},{33,97},{65,1},{97,33},{2,66}... | collective-permute-start | bytes 110600 | tf_op jit(solution)/shard_map/exchange_amplitudes/ppermute | solution.py:44
  13.4 3.3 %collective-permute-done.2.refs_2_ = f32[2,9,512]{2,1,0:T(8,128)S(1)} collective-permute-done((f32[2,9,512]{2,1,0:T(8,128)S(1)}, f32[2,9,512]{2,1,0:T(8,128)S(1)}, u32[]{:S(2)}, u32[]{:S(2)}) %collective-permute-start.2) | collective-permute-done | bytes 36896 | tf_op jit(solution)/shard_map/exchange_amplitudes/ppermute | solution.py:44
  16.7 1.9 %collective-permute-done.3.refs_3_ = f32[2,9,512]{2,1,0:T(8,128)S(1)} collective-permute-done((f32[2,9,512]{2,1,0:T(8,128)S(1)}, f32[2,9,512]{2,1,0:T(8,128)S(1)}, u32[]{:S(2)}, u32[]{:S(2)}) %collective-permute-start.3) | collective-permute-done | bytes 36896 | tf_op jit(solution)/shard_map/exchange_amplitudes/ppermute | solution.py:44
  18.7 2.0 %collective-permute-start.4 = (f32[72,512]{1,0:T(8,128)S(1)}, f32[72,512]{1,0:T(8,128)S(1)}, u32[]{:S(2)}, u32[]{:S(2)}) collective-permute-start(f32[72,512]{1,0:T(8,128)S(1)} %line_up_kernel.1.refs_0_.refs_2_), channel_id=1, source_target_pairs={{0,2},{2,4},{4,6},{6,8},{8,10},{10,12},{12,14},{14,0},{1,3},{3,5},... | collective-permute-start | bytes 442376 | tf_op jit(solution)/shard_map/gather_amplitudes/ppermute | solution.py:48
  20.6 4.0 %collective-permute-start.5 = (f32[72,512]{1,0:T(8,128)S(1)}, f32[72,512]{1,0:T(8,128)S(1)}, u32[]{:S(2)}, u32[]{:S(2)}) collective-permute-start(f32[72,512]{1,0:T(8,128)S(1)} %line_up_kernel.1.refs_0_.refs_2_), channel_id=1, source_target_pairs={{0,14},{2,0},{4,2},{6,4},{8,6},{10,8},{12,10},{14,12},{1,15},{3,1}... | collective-permute-start | bytes 442376 | tf_op jit(solution)/shard_map/gather_amplitudes/ppermute | solution.py:48
  24.7 4.5 %collective-permute-start.6 = (f32[72,512]{1,0:T(8,128)S(1)}, f32[72,512]{1,0:T(8,128)S(1)}, u32[]{:S(2)}, u32[]{:S(2)}) collective-permute-start(f32[72,512]{1,0:T(8,128)S(1)} %line_up_kernel.1.refs_0_.refs_2_), channel_id=1, source_target_pairs={{0,8},{2,10},{4,12},{6,14},{8,0},{10,2},{12,4},{14,6},{1,9},{3,11}... | collective-permute-start | bytes 442376 | tf_op jit(solution)/shard_map/gather_amplitudes/ppermute | solution.py:48
  29.3 5.6 %collective-permute-done.6.refs_4_.refs_3_ = f32[72,512]{1,0:T(8,128)S(1)} collective-permute-done((f32[72,512]{1,0:T(8,128)S(1)}, f32[72,512]{1,0:T(8,128)S(1)}, u32[]{:S(2)}, u32[]{:S(2)}) %collective-permute-start.6) | collective-permute-done | bytes 147488 | tf_op jit(solution)/shard_map/gather_amplitudes/ppermute | solution.py:48
  35.2 2.9 %collective-permute-start.13 = (f32[128,1280]{1,0:T(8,128)S(1)}, f32[128,1280]{1,0:T(8,128)S(1)}, u32[]{:S(2)}, u32[]{:S(2)}) collective-permute-start(f32[128,1280]{1,0:T(8,128)S(1)} %get-tuple-element.60), channel_id=1, source_target_pairs={{0,128},{128,0},{1,129},{129,1},{2,130},{130,2},{3,131},{131,3},{4... | collective-permute-start | bytes 1966088 | tf_op jit(solution)/shard_map/gather_integrals/ppermute | solution.py:44
  39.4 2.8 %collective-permute-start.8 = (f32[144,512]{1,0:T(8,128)S(1)}, f32[144,512]{1,0:T(8,128)S(1)}, u32[]{:S(2)}, u32[]{:S(2)}) collective-permute-start(f32[144,512]{1,0:T(8,128)S(1)} %get-tuple-element.54), channel_id=1, source_target_pairs={{0,12},{2,14},{4,0},{6,2},{8,4},{10,6},{12,8},{14,10},{1,13},{3,15... | collective-permute-start | bytes 884744 | tf_op jit(solution)/shard_map/gather_amplitudes/ppermute | solution.py:48
  42.3 7.3 %collective-permute-done.7.refs_4_ = f32[144,512]{1,0:T(8,128)S(1)} collective-permute-done((f32[144,512]{1,0:T(8,128)S(1)}, f32[144,512]{1,0:T(8,128)S(1)}, u32[]{:S(2)}, u32[]{:S(2)}) %collective-permute-start.7) | collective-permute-done | bytes 294944 | tf_op jit(solution)/shard_map/gather_amplitudes/ppermute | solution.py:48
  49.5 5.5 %collective-permute-done.8.refs_5_ = f32[144,512]{1,0:T(8,128)S(1)} collective-permute-done((f32[144,512]{1,0:T(8,128)S(1)}, f32[144,512]{1,0:T(8,128)S(1)}, u32[]{:S(2)}, u32[]{:S(2)}) %collective-permute-start.8) | collective-permute-done | bytes 294944 | tf_op jit(solution)/shard_map/gather_amplitudes/ppermute | solution.py:48
  55.5 1.6 %theirs_kernel.2 = f32[288,1280]{1,0:T(8,128)S(1)} custom-call(bf16[288,512]{1,0:T(8,128)(2,1)S(1)} %get-tuple-element.57.refs_0_, bf16[288,512]{1,0:T(8,128)(2,1)S(1)} %get-tuple-element.58.refs_1_, f32[256,1280]{1,0:T(8,128)S(1)} %copy-done, f32[256,1280]{1,0:T(8,128)S(1)} %collective-permute-done.9.refs_3_.refs_0_), custom_call_target="tpu_custom_call" | custom-call | flops 1000 | bytes 1000 | tf_op jit(solution)/shard_map/product/theirs_kernel/pallas_call | solution.py:23
  57.4 1.6 %theirs_kernel.3.refs_5_ = f32[288,1280]{1,0:T(8,128)S(1)} custom-call(bf16[288,512]{1,0:T(8,128)(2,1)S(1)} %get-tuple-element.57.refs_0_, bf16[288,512]{1,0:T(8,128)(2,1)S(1)} %get-tuple-element.58.refs_1_, f32[128,1280]{1,0:T(8,128)S(1)} %collective-permute-done.12.refs_2_, f32[128,1280]{1,0:T(8,128)S(1)} %collective-permute-done.13.refs_3_, ...), custom_call_target="tpu_custom_call" | custom-call | flops 1000 | bytes 1000 | tf_op jit(solution)/shard_map/product/theirs_kernel/pallas_call | solution.py:23
  60.7 1.7 %ours_kernel.2 = (f32[144,640]{1,0:T(8,128)S(1)}, f32[144,640]{1,0:T(8,128)S(1)}, f32[144,640]{1,0:T(8,128)S(1)}, f32[144,640]{1,0:T(8,128)S(1)}) custom-call(bf16[288,512]{1,0:T(8,128)(2,1)S(1)} %get-tuple-element.55.refs_0_, bf16[288,512]{1,0:T(8,128)(2,1)S(1)} %get-tuple-element.56.refs_1_, f32[256,1280]{1,0:T(8,128)S(1)} %copy-done, ...), custom_call_target="tpu_custom_call" | custom-call | flops 1000 | bytes 1000 | tf_op jit(solution)/shard_map/product/ours_kernel/pallas_call | solution.py:23
  62.4 1.7 %collective-permute-start.14 = (f32[144,640]{1,0:T(8,128)S(1)}, f32[144,640]{1,0:T(8,128)S(1)}, u32[]{:S(2)}, u32[]{:S(2)}) collective-permute-start(f32[144,640]{1,0:T(8,128)S(1)} %get-tuple-element.62), channel_id=1, source_target_pairs={{0,32},{32,0},{64,96},{96,64},{1,33},{33,1},{65,97},{97,65},{2,34}... | collective-permute-start | bytes 1105928 | tf_op jit(solution)/shard_map/sum_y/ppermute | solution.py:44
  64.1 2.2 %collective-permute-start.15 = (f32[144,640]{1,0:T(8,128)S(1)}, f32[144,640]{1,0:T(8,128)S(1)}, u32[]{:S(2)}, u32[]{:S(2)}) collective-permute-start(f32[144,640]{1,0:T(8,128)S(1)} %get-tuple-element.64), channel_id=1, source_target_pairs={{0,96},{32,64},{64,32},{96,0},{1,97},{33,65},{65,33},{97,1},{2,98}... | collective-permute-start | bytes 1105928 | tf_op jit(solution)/shard_map/sum_y/ppermute | solution.py:44
  66.2 1.7 %ours_kernel.3 = (f32[144,640]{1,0:T(8,128)S(1)}, f32[144,640]{1,0:T(8,128)S(1)}, f32[144,640]{1,0:T(8,128)S(1)}, f32[144,640]{1,0:T(8,128)S(1)}) custom-call(bf16[288,512]{1,0:T(8,128)(2,1)S(1)} %get-tuple-element.55.refs_0_, bf16[288,512]{1,0:T(8,128)(2,1)S(1)} %get-tuple-element.56.refs_1_, f32[128,1280]{1,0:T(8,128)S(1)} %collective-permute-done.12.refs_2_, ...), custom_call_target="tpu_custom_call" | custom-call | flops 1000 | bytes 1000 | tf_op jit(solution)/shard_map/product/ours_kernel/pallas_call | solution.py:23
  69.3 4.6 %collective-permute-done.14.refs_1_ = f32[144,640]{1,0:T(8,128)S(1)} collective-permute-done((f32[144,640]{1,0:T(8,128)S(1)}, f32[144,640]{1,0:T(8,128)S(1)}, u32[]{:S(2)}, u32[]{:S(2)}) %collective-permute-start.14) | collective-permute-done | bytes 368672 | tf_op jit(solution)/shard_map/sum_y/ppermute | solution.py:44
  73.9 2.8 %collective-permute-done.15.refs_3_.refs_4_ = f32[144,640]{1,0:T(8,128)S(1)} collective-permute-done((f32[144,640]{1,0:T(8,128)S(1)}, f32[144,640]{1,0:T(8,128)S(1)}, u32[]{:S(2)}, u32[]{:S(2)}) %collective-permute-start.15) | collective-permute-done | bytes 368672 | tf_op jit(solution)/shard_map/sum_y/ppermute | solution.py:44
  76.8 2.3 %collective-permute-start.17 = (f32[72,640]{1,0:T(8,128)S(1)}, f32[72,640]{1,0:T(8,128)S(1)}, u32[]{:S(2)}, u32[]{:S(2)}) collective-permute-start(f32[72,640]{1,0:T(8,128)S(1)} %get-tuple-element.66), channel_id=1, source_target_pairs={{0,96},{32,64},{64,32},{96,0},{1,97},{33,65},{65,33},{97,1},{2,98}... | collective-permute-start | bytes 552968 | tf_op jit(solution)/shard_map/sum_y/ppermute | solution.py:44
  79.1 2.7 %collective-permute-done.24.refs_1_ = f32[144,640]{1,0:T(8,128)S(1)} collective-permute-done((f32[144,640]{1,0:T(8,128)S(1)}, f32[144,640]{1,0:T(8,128)S(1)}, u32[]{:S(2)}, u32[]{:S(2)}) %collective-permute-start.24) | collective-permute-done | bytes 368672 | tf_op jit(solution)/shard_map/sum_y/ppermute | solution.py:44
  81.8 2.8 %collective-permute-done.25.refs_3_.refs_4_ = f32[144,640]{1,0:T(8,128)S(1)} collective-permute-done((f32[144,640]{1,0:T(8,128)S(1)}, f32[144,640]{1,0:T(8,128)S(1)}, u32[]{:S(2)}, u32[]{:S(2)}) %collective-permute-start.25) | collective-permute-done | bytes 368672 | tf_op jit(solution)/shard_map/sum_y/ppermute | solution.py:44
  84.7 2.3 %collective-permute-start.26 = (f32[72,640]{1,0:T(8,128)S(1)}, f32[72,640]{1,0:T(8,128)S(1)}, u32[]{:S(2)}, u32[]{:S(2)}) collective-permute-start(f32[72,640]{1,0:T(8,128)S(1)} %get-tuple-element.79), channel_id=1, source_target_pairs={{0,96},{32,64},{64,32},{96,0},{1,97},{33,65},{65,33},{97,1},{2,98}... | collective-permute-start | bytes 552968 | tf_op jit(solution)/shard_map/sum_y/ppermute | solution.py:44
  90.6 4.5 %collective-permute-start.21 = (f32[90,128]{1,0:T(8,128)S(1)}, f32[90,128]{1,0:T(8,128)S(1)}, u32[]{:S(2)}, u32[]{:S(2)}) collective-permute-start(f32[90,128]{1,0:T(8,128)S(1)} %get-tuple-element.73), channel_id=1, source_target_pairs={{0,8},{2,10},{4,12},{6,14},{8,0},{10,2},{12,4},{14,6},{1,9},{3,11}... | collective-permute-start | bytes 138248 | tf_op jit(solution)/shard_map/to_owner/ppermute | solution.py:48
  95.2 3.5 %collective-permute-start.28 = (f32[2,90,128]{2,1,0:T(8,128)S(1)}, f32[2,90,128]{2,1,0:T(8,128)S(1)}, u32[]{:S(2)}, u32[]{:S(2)}) collective-permute-start(f32[2,90,128]{2,1,0:T(8,128)S(1)} %get-tuple-element.82), channel_id=1, source_target_pairs={{0,14},{2,0},{4,2},{6,4},{8,6},{10,8},{12,10},{14,12},{1,15},{3,1}... | collective-permute-start | bytes 276488 | tf_op jit(solution)/shard_map/to_owner/ppermute | solution.py:48
  100.0 3.6 %collective-permute-start.30 = (f32[90,128]{1,0:T(8,128)S(1)}, f32[90,128]{1,0:T(8,128)S(1)}, u32[]{:S(2)}, u32[]{:S(2)}) collective-permute-start(f32[90,128]{1,0:T(8,128)S(1)} %get-tuple-element.86), channel_id=1, source_target_pairs={{0,8},{2,10},{4,12},{6,14},{8,0},{10,2},{12,4},{14,6},{1,9},{3,11}... | collective-permute-start | bytes 138248 | tf_op jit(solution)/shard_map/to_owner/ppermute | solution.py:48
  103.7 2.8 %collective-permute-start.22 = (f32[2,90,128]{2,1,0:T(8,128)S(1)}, f32[2,90,128]{2,1,0:T(8,128)S(1)}, u32[]{:S(2)}, u32[]{:S(2)}) collective-permute-start(f32[2,90,128]{2,1,0:T(8,128)S(1)} %get-tuple-element.74), channel_id=1, source_target_pairs={{0,12},{2,14},{4,0},{6,2},{8,4},{10,6},{12,8},{14,10},{1,13},{3,15... | collective-permute-start | bytes 276488 | tf_op jit(solution)/shard_map/to_owner/ppermute | solution.py:48
  108.3 4.2 %collective-permute-start.31 = (f32[2,90,128]{2,1,0:T(8,128)S(1)}, f32[2,90,128]{2,1,0:T(8,128)S(1)}, u32[]{:S(2)}, u32[]{:S(2)}) collective-permute-start(f32[2,90,128]{2,1,0:T(8,128)S(1)} %get-tuple-element.87), channel_id=1, source_target_pairs={{0,12},{2,14},{4,0},{6,2},{8,4},{10,6},{12,8},{14,10},{1,13},{3,15... | collective-permute-start | bytes 276488 | tf_op jit(solution)/shard_map/to_owner/ppermute | solution.py:48
  112.5 2.7 %collective-permute-done.23.refs_4_ = f32[2,90,128]{2,1,0:T(8,128)S(1)} collective-permute-done((f32[2,90,128]{2,1,0:T(8,128)S(1)}, f32[2,90,128]{2,1,0:T(8,128)S(1)}, u32[]{:S(2)}, u32[]{:S(2)}) %collective-permute-start.23) | collective-permute-done | bytes 92192 | tf_op jit(solution)/shard_map/to_owner/ppermute | solution.py:48
  115.6 4.5 %collective-permute-done.32.refs_10_ = f32[2,90,128]{2,1,0:T(8,128)S(1)} collective-permute-done((f32[2,90,128]{2,1,0:T(8,128)S(1)}, f32[2,90,128]{2,1,0:T(8,128)S(1)}, u32[]{:S(2)}, u32[]{:S(2)}) %collective-permute-start.32) | collective-permute-done | bytes 92192 | tf_op jit(solution)/shard_map/to_owner/ppermute | solution.py:48
  (66 shorter events, 20.8 us)
Async XLA Ops:
  0.0 34.9 %collective-permute-start.9 = (f32[256,1280]{1,0:T(8,128)}, f32[256,1280]{1,0:T(8,128)S(1)}, u32[]{:S(2)}, u32[]{:S(2)}) collective-permute-start(f32[256,1280]{1,0:T(8,128)} %refs_2_.3), channel_id=1, source_target_pairs={{0,128},{128,0},{1,129},{129,1},{2,130},{130,2},{3,131},{131,3},{4... | collective-permute-start | bytes 3932168 | tf_op jit(solution)/shard_map/gather_integrals/ppermute | solution.py:44
  2.3 32.7 %collective-permute-start.11 = (f32[256,1280]{1,0:T(8,128)}, f32[256,1280]{1,0:T(8,128)S(1)}, u32[]{:S(2)}, u32[]{:S(2)}) collective-permute-start(f32[256,1280]{1,0:T(8,128)} %refs_2_.3), channel_id=1, source_target_pairs={{0,129},{1,128},{128,1},{129,0},{2,131},{3,130},{130,3},{131,2},{4... | collective-permute-start | bytes 3932168 | tf_op jit(solution)/shard_map/gather_integrals/ppermute | solution.py:44
  8.6 4.8 %collective-permute-start.1 = (f32[2,9,512]{2,1,0:T(8,128)S(1)}, f32[2,9,512]{2,1,0:T(8,128)S(1)}, u32[]{:S(2)}, u32[]{:S(2)}) collective-permute-start(f32[2,9,512]{2,1,0:T(8,128)S(1)} %get-tuple-element.50), channel_id=1, source_target_pairs={{0,32},{32,0},{64,96},{96,64},{1,33},{33,1},{65,97},{97,65},{2,34}... | collective-permute-start | bytes 110600 | tf_op jit(solution)/shard_map/exchange_amplitudes/ppermute | solution.py:44
  10.2 6.4 %collective-permute-start.2 = (f32[2,9,512]{2,1,0:T(8,128)S(1)}, f32[2,9,512]{2,1,0:T(8,128)S(1)}, u32[]{:S(2)}, u32[]{:S(2)}) collective-permute-start(f32[2,9,512]{2,1,0:T(8,128)S(1)} %get-tuple-element.51), channel_id=1, source_target_pairs={{0,64},{32,96},{64,0},{96,32},{1,65},{33,97},{65,1},{97,33},{2,66}... | collective-permute-start | bytes 110600 | tf_op jit(solution)/shard_map/exchange_amplitudes/ppermute | solution.py:44
  13.1 5.5 %collective-permute-start.3 = (f32[2,9,512]{2,1,0:T(8,128)S(1)}, f32[2,9,512]{2,1,0:T(8,128)S(1)}, u32[]{:S(2)}, u32[]{:S(2)}) collective-permute-start(f32[2,9,512]{2,1,0:T(8,128)S(1)} %get-tuple-element.52), channel_id=1, source_target_pairs={{0,96},{32,64},{64,32},{96,0},{1,97},{33,65},{65,33},{97,1},{2,98}... | collective-permute-start | bytes 110600 | tf_op jit(solution)/shard_map/exchange_amplitudes/ppermute | solution.py:44
  18.7 10.6 %collective-permute-start.4 = (f32[72,512]{1,0:T(8,128)S(1)}, f32[72,512]{1,0:T(8,128)S(1)}, u32[]{:S(2)}, u32[]{:S(2)}) collective-permute-start(f32[72,512]{1,0:T(8,128)S(1)} %line_up_kernel.1.refs_0_.refs_2_), channel_id=1, source_target_pairs={{0,2},{2,4},{4,6},{6,8},{8,10},{10,12},{12,14},{14,0},{1,3},{3,5},... | collective-permute-start | bytes 442376 | tf_op jit(solution)/shard_map/gather_amplitudes/ppermute | solution.py:48
  20.6 8.6 %collective-permute-start.5 = (f32[72,512]{1,0:T(8,128)S(1)}, f32[72,512]{1,0:T(8,128)S(1)}, u32[]{:S(2)}, u32[]{:S(2)}) collective-permute-start(f32[72,512]{1,0:T(8,128)S(1)} %line_up_kernel.1.refs_0_.refs_2_), channel_id=1, source_target_pairs={{0,14},{2,0},{4,2},{6,4},{8,6},{10,8},{12,10},{14,12},{1,15},{3,1}... | collective-permute-start | bytes 442376 | tf_op jit(solution)/shard_map/gather_amplitudes/ppermute | solution.py:48
  24.7 10.2 %collective-permute-start.6 = (f32[72,512]{1,0:T(8,128)S(1)}, f32[72,512]{1,0:T(8,128)S(1)}, u32[]{:S(2)}, u32[]{:S(2)}) collective-permute-start(f32[72,512]{1,0:T(8,128)S(1)} %line_up_kernel.1.refs_0_.refs_2_), channel_id=1, source_target_pairs={{0,8},{2,10},{4,12},{6,14},{8,0},{10,2},{12,4},{14,6},{1,9},{3,11}... | collective-permute-start | bytes 442376 | tf_op jit(solution)/shard_map/gather_amplitudes/ppermute | solution.py:48
  35.1 22.4 %collective-permute-start.12 = (f32[128,1280]{1,0:T(8,128)S(1)}, f32[128,1280]{1,0:T(8,128)S(1)}, u32[]{:S(2)}, u32[]{:S(2)}) collective-permute-start(f32[128,1280]{1,0:T(8,128)S(1)} %get-tuple-element.59), channel_id=1, source_target_pairs={{0,129},{1,128},{128,1},{129,0},{2,131},{3,130},{130,3},{131,2},{4... | collective-permute-start | bytes 1966088 | tf_op jit(solution)/shard_map/gather_integrals/ppermute | solution.py:44
  35.2 22.3 %collective-permute-start.13 = (f32[128,1280]{1,0:T(8,128)S(1)}, f32[128,1280]{1,0:T(8,128)S(1)}, u32[]{:S(2)}, u32[]{:S(2)}) collective-permute-start(f32[128,1280]{1,0:T(8,128)S(1)} %get-tuple-element.60), channel_id=1, source_target_pairs={{0,128},{128,0},{1,129},{129,1},{2,130},{130,2},{3,131},{131,3},{4... | collective-permute-start | bytes 1966088 | tf_op jit(solution)/shard_map/gather_integrals/ppermute | solution.py:44
  38.0 11.5 %collective-permute-start.7 = (f32[144,512]{1,0:T(8,128)S(1)}, f32[144,512]{1,0:T(8,128)S(1)}, u32[]{:S(2)}, u32[]{:S(2)}) collective-permute-start(f32[144,512]{1,0:T(8,128)S(1)} %get-tuple-element.53.refs_2_), channel_id=1, source_target_pairs={{0,4},{2,6},{4,8},{6,10},{8,12},{10,14},{12,0},{14,2},{1,5},{3,7},... | collective-permute-start | bytes 884744 | tf_op jit(solution)/shard_map/gather_amplitudes/ppermute | solution.py:48
  39.4 15.6 %collective-permute-start.8 = (f32[144,512]{1,0:T(8,128)S(1)}, f32[144,512]{1,0:T(8,128)S(1)}, u32[]{:S(2)}, u32[]{:S(2)}) collective-permute-start(f32[144,512]{1,0:T(8,128)S(1)} %get-tuple-element.54), channel_id=1, source_target_pairs={{0,12},{2,14},{4,0},{6,2},{8,4},{10,6},{12,8},{14,10},{1,13},{3,15... | collective-permute-start | bytes 884744 | tf_op jit(solution)/shard_map/gather_amplitudes/ppermute | solution.py:48
  57.1 3.5 %collective-permute-start.10 = (f32[288,1280]{1,0:T(8,128)S(1)}, f32[288,1280]{1,0:T(8,128)S(1)}, u32[]{:S(2)}, u32[]{:S(2)}) collective-permute-start(f32[288,1280]{1,0:T(8,128)S(1)} %theirs_kernel.2), channel_id=1, source_target_pairs={{0,16},{16,0},{1,17},{17,1},{2,18},{18,2},{3,19},{19,3},{4,20},{20... | collective-permute-start | bytes 4423688 | tf_op jit(solution)/shard_map/sum_core/ppermute | solution.py:44
  59.1 7.2 %collective-permute-start.16 = (f32[288,1280]{1,0:T(8,128)S(1)}, f32[288,1280]{1,0:T(8,128)S(1)}, u32[]{:S(2)}, u32[]{:S(2)}) collective-permute-start(f32[288,1280]{1,0:T(8,128)S(1)} %theirs_kernel.3.refs_5_), channel_id=1, source_target_pairs={{0,16},{16,0},{1,17},{17,1},{2,18},{18,2},{3,19},{19,3},{4,20},{20... | collective-permute-start | bytes 4423688 | tf_op jit(solution)/shard_map/sum_core/ppermute | solution.py:44
  62.4 11.5 %collective-permute-start.14 = (f32[144,640]{1,0:T(8,128)S(1)}, f32[144,640]{1,0:T(8,128)S(1)}, u32[]{:S(2)}, u32[]{:S(2)}) collective-permute-start(f32[144,640]{1,0:T(8,128)S(1)} %get-tuple-element.62), channel_id=1, source_target_pairs={{0,32},{32,0},{64,96},{96,64},{1,33},{33,1},{65,97},{97,65},{2,34}... | collective-permute-start | bytes 1105928 | tf_op jit(solution)/shard_map/sum_y/ppermute | solution.py:44
  64.1 12.7 %collective-permute-start.15 = (f32[144,640]{1,0:T(8,128)S(1)}, f32[144,640]{1,0:T(8,128)S(1)}, u32[]{:S(2)}, u32[]{:S(2)}) collective-permute-start(f32[144,640]{1,0:T(8,128)S(1)} %get-tuple-element.64), channel_id=1, source_target_pairs={{0,96},{32,64},{64,32},{96,0},{1,97},{33,65},{65,33},{97,1},{2,98}... | collective-permute-start | bytes 1105928 | tf_op jit(solution)/shard_map/sum_y/ppermute | solution.py:44
  68.0 13.9 %collective-permute-start.24 = (f32[144,640]{1,0:T(8,128)S(1)}, f32[144,640]{1,0:T(8,128)S(1)}, u32[]{:S(2)}, u32[]{:S(2)}) collective-permute-start(f32[144,640]{1,0:T(8,128)S(1)} %get-tuple-element.65.refs_4_), channel_id=1, source_target_pairs={{0,32},{32,0},{64,96},{96,64},{1,33},{33,1},{65,97},{97,65},{2,34}... | collective-permute-start | bytes 1105928 | tf_op jit(solution)/shard_map/sum_y/ppermute | solution.py:44
  68.7 15.9 %collective-permute-start.25 = (f32[144,640]{1,0:T(8,128)S(1)}, f32[144,640]{1,0:T(8,128)S(1)}, u32[]{:S(2)}, u32[]{:S(2)}) collective-permute-start(f32[144,640]{1,0:T(8,128)S(1)} %get-tuple-element.78), channel_id=1, source_target_pairs={{0,96},{32,64},{64,32},{96,0},{1,97},{33,65},{65,33},{97,1},{2,98}... | collective-permute-start | bytes 1105928 | tf_op jit(solution)/shard_map/sum_y/ppermute | solution.py:44
  76.8 11.6 %collective-permute-start.17 = (f32[72,640]{1,0:T(8,128)S(1)}, f32[72,640]{1,0:T(8,128)S(1)}, u32[]{:S(2)}, u32[]{:S(2)}) collective-permute-start(f32[72,640]{1,0:T(8,128)S(1)} %get-tuple-element.66), channel_id=1, source_target_pairs={{0,96},{32,64},{64,32},{96,0},{1,97},{33,65},{65,33},{97,1},{2,98}... | collective-permute-start | bytes 552968 | tf_op jit(solution)/shard_map/sum_y/ppermute | solution.py:44
  79.1 9.4 %collective-permute-start.18 = (f32[72,640]{1,0:T(8,128)S(1)}, f32[72,640]{1,0:T(8,128)S(1)}, u32[]{:S(2)}, u32[]{:S(2)}) collective-permute-start(f32[72,640]{1,0:T(8,128)S(1)} %get-tuple-element.67), channel_id=1, source_target_pairs={{0,32},{32,0},{64,96},{96,64},{1,33},{33,1},{65,97},{97,65},{2,34}... | collective-permute-start | bytes 552968 | tf_op jit(solution)/shard_map/sum_y/ppermute | solution.py:44
  84.7 10.4 %collective-permute-start.26 = (f32[72,640]{1,0:T(8,128)S(1)}, f32[72,640]{1,0:T(8,128)S(1)}, u32[]{:S(2)}, u32[]{:S(2)}) collective-permute-start(f32[72,640]{1,0:T(8,128)S(1)} %get-tuple-element.79), channel_id=1, source_target_pairs={{0,96},{32,64},{64,32},{96,0},{1,97},{33,65},{65,33},{97,1},{2,98}... | collective-permute-start | bytes 552968 | tf_op jit(solution)/shard_map/sum_y/ppermute | solution.py:44
  87.0 8.2 %collective-permute-start.27 = (f32[72,640]{1,0:T(8,128)S(1)}, f32[72,640]{1,0:T(8,128)S(1)}, u32[]{:S(2)}, u32[]{:S(2)}) collective-permute-start(f32[72,640]{1,0:T(8,128)S(1)} %get-tuple-element.80), channel_id=1, source_target_pairs={{0,32},{32,0},{64,96},{96,64},{1,33},{33,1},{65,97},{97,65},{2,34}... | collective-permute-start | bytes 552968 | tf_op jit(solution)/shard_map/sum_y/ppermute | solution.py:44
  88.5 15.1 %collective-permute-start.19 = (f32[2,90,128]{2,1,0:T(8,128)S(1)}, f32[2,90,128]{2,1,0:T(8,128)S(1)}, u32[]{:S(2)}, u32[]{:S(2)}) collective-permute-start(f32[2,90,128]{2,1,0:T(8,128)S(1)} %get-tuple-element.69), channel_id=1, source_target_pairs={{0,14},{2,0},{4,2},{6,4},{8,6},{10,8},{12,10},{14,12},{1,15},{3,1}... | collective-permute-start | bytes 276488 | tf_op jit(solution)/shard_map/to_owner/ppermute | solution.py:48
  89.2 14.4 %collective-permute-start.20 = (f32[2,90,128]{2,1,0:T(8,128)S(1)}, f32[2,90,128]{2,1,0:T(8,128)S(1)}, u32[]{:S(2)}, u32[]{:S(2)}) collective-permute-start(f32[2,90,128]{2,1,0:T(8,128)S(1)} %get-tuple-element.72), channel_id=1, source_target_pairs={{0,2},{2,4},{4,6},{6,8},{8,10},{10,12},{12,14},{14,0},{1,3},{3,5},... | collective-permute-start | bytes 276488 | tf_op jit(solution)/shard_map/to_owner/ppermute | solution.py:48
  90.6 9.4 %collective-permute-start.21 = (f32[90,128]{1,0:T(8,128)S(1)}, f32[90,128]{1,0:T(8,128)S(1)}, u32[]{:S(2)}, u32[]{:S(2)}) collective-permute-start(f32[90,128]{1,0:T(8,128)S(1)} %get-tuple-element.73), channel_id=1, source_target_pairs={{0,8},{2,10},{4,12},{6,14},{8,0},{10,2},{12,4},{14,6},{1,9},{3,11}... | collective-permute-start | bytes 138248 | tf_op jit(solution)/shard_map/to_owner/ppermute | solution.py:48
  95.2 13.0 %collective-permute-start.28 = (f32[2,90,128]{2,1,0:T(8,128)S(1)}, f32[2,90,128]{2,1,0:T(8,128)S(1)}, u32[]{:S(2)}, u32[]{:S(2)}) collective-permute-start(f32[2,90,128]{2,1,0:T(8,128)S(1)} %get-tuple-element.82), channel_id=1, source_target_pairs={{0,14},{2,0},{4,2},{6,4},{8,6},{10,8},{12,10},{14,12},{1,15},{3,1}... | collective-permute-start | bytes 276488 | tf_op jit(solution)/shard_map/to_owner/ppermute | solution.py:48
  98.8 9.5 %collective-permute-start.29 = (f32[2,90,128]{2,1,0:T(8,128)S(1)}, f32[2,90,128]{2,1,0:T(8,128)S(1)}, u32[]{:S(2)}, u32[]{:S(2)}) collective-permute-start(f32[2,90,128]{2,1,0:T(8,128)S(1)} %get-tuple-element.85), channel_id=1, source_target_pairs={{0,2},{2,4},{4,6},{6,8},{8,10},{10,12},{12,14},{14,0},{1,3},{3,5},... | collective-permute-start | bytes 276488 | tf_op jit(solution)/shard_map/to_owner/ppermute | solution.py:48
  100.0 8.2 %collective-permute-start.30 = (f32[90,128]{1,0:T(8,128)S(1)}, f32[90,128]{1,0:T(8,128)S(1)}, u32[]{:S(2)}, u32[]{:S(2)}) collective-permute-start(f32[90,128]{1,0:T(8,128)S(1)} %get-tuple-element.86), channel_id=1, source_target_pairs={{0,8},{2,10},{4,12},{6,14},{8,0},{10,2},{12,4},{14,6},{1,9},{3,11}... | collective-permute-start | bytes 138248 | tf_op jit(solution)/shard_map/to_owner/ppermute | solution.py:48
  103.7 8.8 %collective-permute-start.22 = (f32[2,90,128]{2,1,0:T(8,128)S(1)}, f32[2,90,128]{2,1,0:T(8,128)S(1)}, u32[]{:S(2)}, u32[]{:S(2)}) collective-permute-start(f32[2,90,128]{2,1,0:T(8,128)S(1)} %get-tuple-element.74), channel_id=1, source_target_pairs={{0,12},{2,14},{4,0},{6,2},{8,4},{10,6},{12,8},{14,10},{1,13},{3,15... | collective-permute-start | bytes 276488 | tf_op jit(solution)/shard_map/to_owner/ppermute | solution.py:48
  106.5 8.7 %collective-permute-start.23 = (f32[2,90,128]{2,1,0:T(8,128)S(1)}, f32[2,90,128]{2,1,0:T(8,128)S(1)}, u32[]{:S(2)}, u32[]{:S(2)}) collective-permute-start(f32[2,90,128]{2,1,0:T(8,128)S(1)} %get-tuple-element.75), channel_id=1, source_target_pairs={{0,4},{2,6},{4,8},{6,10},{8,12},{10,14},{12,0},{14,2},{1,5},{3,7},... | collective-permute-start | bytes 276488 | tf_op jit(solution)/shard_map/to_owner/ppermute | solution.py:48
  108.3 7.3 %collective-permute-start.31 = (f32[2,90,128]{2,1,0:T(8,128)S(1)}, f32[2,90,128]{2,1,0:T(8,128)S(1)}, u32[]{:S(2)}, u32[]{:S(2)}) collective-permute-start(f32[2,90,128]{2,1,0:T(8,128)S(1)} %get-tuple-element.87), channel_id=1, source_target_pairs={{0,12},{2,14},{4,0},{6,2},{8,4},{10,6},{12,8},{14,10},{1,13},{3,15... | collective-permute-start | bytes 276488 | tf_op jit(solution)/shard_map/to_owner/ppermute | solution.py:48
  112.4 7.6 %collective-permute-start.32 = (f32[2,90,128]{2,1,0:T(8,128)S(1)}, f32[2,90,128]{2,1,0:T(8,128)S(1)}, u32[]{:S(2)}, u32[]{:S(2)}) collective-permute-start(f32[2,90,128]{2,1,0:T(8,128)S(1)} %get-tuple-element.88), channel_id=1, source_target_pairs={{0,4},{2,6},{4,8},{6,10},{8,12},{10,14},{12,0},{14,2},{1,5},{3,7},... | collective-permute-start | bytes 276488 | tf_op jit(solution)/shard_map/to_owner/ppermute | solution.py:48
  (8 other events, 80.3 us)

commit v3 on v2

--- a/solution.py
+++ b/solution.py
@@ -89,7 +89,6 @@
         out_specs=[VMEM, VMEM],
         scratch_shapes=[pltpu.VMEM((no * ni, width), jnp.float32)],
         cost_estimate=CHEAP,
-        compiler_params=pltpu.CompilerParams(vmem_limit_bytes=8 * 2**20),
     )(occ_start, vir_start, block_mask, amplitudes)
 
 
@@ -117,32 +116,29 @@
     return call(line_up_kernel, f32(8 * nr, depth), rows)
 
 
-def pair_up_kernel(a, b, c, d, left, right):
-    n = a.shape[0]
-    left[:n], left[n:] = a[...], b[...]
-    right[:n], right[n:] = c[...], d[...]
-
-
-def pair_up(mine, down1, up1, across):
-    n, depth = mine.shape
-    return call(pair_up_kernel, [f32(2 * n, depth)] * 2, (mine, down1, mine, up1), (across,))
-
-
-def pass_on_kernel(two, up1, six, down1, up, down):
-    up[0], up[1] = two[...], up1[1]
-    down[0], down[1] = six[...], down1[1]
-
-
-def pass_on(two, up1, six, down1, across):
-    return call(pass_on_kernel, [f32(*up1.shape)] * 2, (two, up1, six, down1), (across,))
+def relay_kernel(d1, u1, d2, u2, down, up):
+    n = d1.shape[0]
+    cut = down.shape[0] - n
+    down[:n, :], down[n:, :] = d1[...], d2[:cut, :]
+    up[:n, :], up[n:, :] = u1[...], u2[cut:, :]
+
+
+def relay(d1, u1, d2, u2):
+    n, depth = d1.shape
+    cut = n // 16 * 8 + 8
+    outs = [f32(n + cut, depth), f32(2 * n - cut, depth)]
+    return call(relay_kernel, outs, (d1, u1, d2, u2))
 
 
 def order_kernel(*refs):
-    own, down1, up1, across, down, up = refs[:6]
-    highs, lows, held = (refs[6], refs[8]), (refs[7], refs[9]), refs[10]
+    own, d1, u1, d2, u2, down, up = refs[:7]
+    highs, lows, (held, across) = (refs[7], refs[9]), (refs[8], refs[10]), refs[11:]
     n = own.shape[0]
     nr = n // 8
-    source = [(own, 0), (down1, 0), (down, 0), (down, n), (across, 0), (up, n), (up, 0), (up1, 0)]
+    cut = down.shape[0] - n
+    across[:cut, :] = down[n:, :]
+    across[cut:, :] = up[n:, :]
+    source = [(own, 0), (d1, 0), (d2, 0), (down, 0), (across, 0), (up, 0), (u2, 0), (u1, 0)]
     for dc in range(2):
         for e in range(4):
             for d, (ref, base) in enumerate(source):
@@ -158,7 +154,7 @@
 def order_rows(*blocks):
     n, depth = blocks[0].shape
     part = jax.ShapeDtypeStruct((4 * n, depth), jnp.bfloat16)
-    return call(order_kernel, [part] * 4, blocks, scratch=[pltpu.VMEM((4 * n, depth), jnp.float32)])
+    return call(order_kernel, [part] * 4, blocks, scratch=[pltpu.VMEM((k * n, depth), jnp.float32) for k in (4, 1)])
 
 
 def halve_kernel(a, b, first, second):
@@ -230,51 +226,46 @@
 
 
 def finish_kernel(*refs):
-    sides, outs = (refs[:3], refs[3:6]), refs[6:]
-    own, up1, down1, across, two, six = outs
-    group, width = sides[0][2].shape
+    out_ref = refs[12]
+    group, width = refs[2].shape
     nr = group // NZ
-    where = [own, (up1, 0), two, (up1, 1), across, (down1, 1), six, (down1, 0)]
-    for s, (keep, got, last) in enumerate(sides):
-        first = 0 if s == 0 else group
+    z = lax.axis_index("z")
+    for k in range(4):
+        keep, got, last = refs[3 * k : 3 * k + 3]
+        first = 0 if k % 2 == 0 else group
         value = keep[:group, :] + got[first : first + group, :] + last[...]
         for d in range(NZ):
+            where = lax.rem(z + NZ - d, NZ)
             for j in range(width // 128):
-                at = (s * (width // 128) + j) * nr
+                at = (k * (width // 128) + j) * nr
                 tile = value[d * nr : (d + 1) * nr, j * 128 : (j + 1) * 128]
-                if isinstance(where[d], tuple):
-                    where[d][0][where[d][1], at : at + nr, :] = tile
-                else:
-                    where[d][at : at + nr, :] = tile
+                out_ref[where, at : at + nr, :] = tile
 
 
 def finish(*args):
     group, width = args[2].shape
-    rows = 2 * width // 128 * (group // NZ)
-    one, two = f32(rows, 128), f32(2, rows, 128)
-    return call(finish_kernel, [one, two, two, one, one, one], args)
-
-
-def scale_kernel(*refs):
-    halves, (occ_ref, vir_ref, out_ref) = (refs[:6], refs[6:12]), refs[12:]
-    z, xh = lax.axis_index("z"), lax.axis_index("xh")
+    return call(finish_kernel, f32(NZ, 4 * width // 128 * (group // NZ), 128), args)
+
+
+def scale_kernel(got_ref, occ_ref, vir_ref, out_ref):
+    xh = lax.axis_index("xh")
     no, ni, _ = out_ref.shape
     nr = no * ni
-    tiles = refs[0].shape[0] // nr
-    for h, (own, up1, up, across, down, down1) in enumerate(halves):
-        source = [own, up1.at[0], up.at[0], up.at[1], across, down.at[1], down.at[0], down1.at[0]]
-        for d, ref in enumerate(source):
-            start = (lax.rem(z + d, NZ) * 2 + (xh ^ h)) * tiles
+    tiles = got_ref.shape[1] // (2 * nr)
+    for d in range(NZ):
+        for h in range(2):
+            start = (d * 2 + (xh ^ h)) * tiles
             for j in range(tiles):
+                at = (h * tiles + j) * nr
                 cols = pl.ds(pl.multiple_of((start + j) * 128, 128), 128)
-                value = ref[j * nr : (j + 1) * nr, :] / (occ_ref[...] - vir_ref[:, cols])
+                value = got_ref[d, at : at + nr, :] / (occ_ref[...] - vir_ref[:, cols])
                 for oo in range(no):
                     out_ref[oo, :, cols] = value[oo * ni : (oo + 1) * ni]
 
 
-def scale(near, far, occ_energy, vir_energy):
+def scale(got, occ_energy, vir_energy):
     no, ni = occ_energy.shape
-    operands = (*near, *far, occ_energy.reshape(no * ni, 1), vir_energy[None, :])
+    operands = (got, occ_energy.reshape(no * ni, 1), vir_energy[None, :])
     return call(scale_kernel, f32(no, ni, vir_energy.shape[0]), operands)
 
 
@@ -288,16 +279,19 @@
         rows = [pair[0]] + [swap(pair[e], "y", e) for e in (1, 2, 3)]
         mine = line_up(rows)
     with jax.named_scope("gather_amplitudes"):
-        across, down1, up1 = along_z(mine, 4), along_z(mine, 1), along_z(mine, 7)
-        pairs = pair_up(mine, down1, up1, across)
+        d2, u2 = along_z(mine, 2), along_z(mine, 6)
+        d1, u1 = along_z(mine, 1), along_z(mine, 7)
+        pairs = relay(d1, u1, d2, u2)
         down, up = along_z(pairs[0], 2), along_z(pairs[1], 6)
-        ours_high, ours_low, theirs_high, theirs_low = order_rows(mine, down1, up1, across, down, up)
+        parts = order_rows(mine, d1, u1, d2, u2, down, up)
+        ours_high, ours_low, theirs_high, theirs_low = parts
     with jax.named_scope("gather_integrals"):
         first, second = halve(xl, d, after=(pairs[0],))
         first, second = swap(first, ("xl", "xh"), 3), swap(second, "xl", 1)
     pieces = ((integrals, xl), (first, second, d))
     with jax.named_scope("product"):
-        theirs = [product(theirs_high, theirs_low, p) for p in pieces]
+        theirs = [product(theirs_high, theirs_low, pieces[0])]
+        theirs.append(product(theirs_high, theirs_low, pieces[1]))
     with jax.named_scope("sum_core"):
         other = [swap(t, "core", 1) for t in theirs]
     with jax.named_scope("product"):
@@ -305,21 +299,19 @@
         sums.append(product(ours_high, ours_low, pieces[1], other[1]))
     with jax.named_scope("sum_y"):
         got = [(swap(a, "y", 1), swap(b, "y", 3)) for a, _, b, _ in sums]
-    halves = []
-    for h in range(2):
-        _, keep_a, _, keep_b = sums[h]
-        got_a, got_b = got[h]
-        with jax.named_scope("sum_y"):
+    ends = []
+    with jax.named_scope("sum_y"):
+        for h in range(2):
+            _, keep_a, _, keep_b = sums[h]
+            got_a, got_b = got[h]
             send_a, send_b = middle(keep_a, got_a, keep_b, got_b, after=(sums[1][0],) * (1 - h))
             last_a, last_b = swap(send_a, "y", 3), swap(send_b, "y", 1)
-            own, up1, down1, across, two, six = finish(keep_a, got_a, last_a, keep_b, got_b, last_b)
-        with jax.named_scope("to_owner"):
-            across, up1, down1 = along_z(across, 4), along_z(up1, 7), along_z(down1, 1)
-            up, down = pass_on(two, up1, six, down1, across)
-            up, down = along_z(up, 6), along_z(down, 2)
-            halves.append((own, up1, up, across, down, down1))
+            ends += [keep_a, got_a, last_a, keep_b, got_b, last_b]
+        piece = finish(*ends)
+    with jax.named_scope("to_owner"):
+        piece = lax.all_to_all(piece, "z", split_axis=0, concat_axis=0, tiled=True)
     with jax.named_scope("scale"):
-        return scale(*halves, occ_energy, vir_energy)
+        return scale(piece, occ_energy, vir_energy)
 
 
 def solution(mesh):

time: 122 us -> 117 us (0.959)
  starting transfers between devices: 56.8 us -> 40.4 us
  waiting for transfers between devices: 50.9 us -> 62.5 us
  local copies, waits for them, and re-layouts: 3.02 us -> 0.99 us
  Pallas kernels: 10.5 us -> 12.4 us
    ppermute x15 -> x6, starting transfers between devices: 35.7 us -> 14.2 us  [along_z(): return lax.ppermute(x, 'z', [(i, (i + d) % NZ) for i in range(NZ)])]
    all_to_all x0 -> x1, waiting for transfers between devices: none -> 19.3 us  [on_device(): piece = lax.all_to_all(piece, 'z', split_axis=0, concat_axis=0, tiled=True)]
    ppermute x15 -> x6, waiting for transfers between devices: 28.8 us -> 16.9 us  [along_z(): return lax.ppermute(x, 'z', [(i, (i + d) % NZ) for i in range(NZ)])]
    all_to_all x0 -> x1, starting transfers between devices: none -> 5.58 us  [on_device(): piece = lax.all_to_all(piece, 'z', split_axis=0, concat_axis=0, tiled=True)]
    ppermute x18, waiting for transfers between devices: 22.1 us -> 26.3 us  [swap(): return lax.ppermute(x, axes, [(i, i ^ bits) for i in range(n)])]
    unnamed x14 -> x8, local copies, waits for them, and re-layouts: 2.94 us -> 0.92 us
    pallas_call x16 -> x13, Pallas kernels: 9.04 us -> 9.89 us  [call(): pl.pallas_call(body, out_shape=out_shape, in_specs=[VMEM] * len(operands)...]
  transfers between devices with their start and end apart: 33 -> 25, of which waited for: 18 -> 17; matrix products, arithmetic and copies ran while one was open for 0% -> 0% of each run, Pallas kernels for 7% -> 8%
where the time goes in v3:
time: 117 us; the launch traced here: 116 us
  waiting for transfers between devices  62.5 us (53%)
  starting transfers between devices  40.4 us (35%)
  Pallas kernels  12.4 us (11%)
    ppermute x18, waiting for transfers between devices, swap(): return lax.ppermute(x, axes, [(i, i ^ bits) for i in range(n)])  26.3 us
    ppermute x18, starting transfers between devices, swap(): return lax.ppermute(x, axes, [(i, i ^ bits) for i in range(n)])  20.6 us
    all_to_all x1, waiting for transfers between devices, on_device(): piece = lax.all_to_all(piece, 'z', split_axis=0, concat_axis=0, tiled=True)  19.3 us
    ppermute x6, waiting for transfers between devices, along_z(): return lax.ppermute(x, 'z', [(i, (i + d) % NZ) for i in range(NZ)])  16.9 us
    ppermute x6, starting transfers between devices, along_z(): return lax.ppermute(x, 'z', [(i, (i + d) % NZ) for i in range(NZ)])  14.2 us
    pallas_call x13, Pallas kernels, call(): pl.pallas_call(body, out_shape=out_shape, in_specs=[VMEM] * len(operands)...  9.89 us
    all_to_all x1, starting transfers between devices, on_device(): piece = lax.all_to_all(piece, 'z', split_axis=0, concat_axis=0, tiled=True)  5.58 us
    pallas_call x1, Pallas kernels, mask_rows(): pl.pallas_call(mask_kernel, out_shape=[half, half], in_specs=[smem, smem,...  2.51 us
  transfers between devices with their start and end apart: 25, of which 17 were waited for; matrix products, arithmetic and copies ran while one was open for 0% of the time, Pallas kernels for 8%

profile of v3, /device:TPU:2, one launch (start us, length us, event | category | flops | bytes accessed | tf_op | source)
XLA Modules:
  0.0 116.4 jit_solution(9567906474514460756)
XLA Ops:
  0.0 2.3 %collective-permute-start.10 = (f32[256,1280]{1,0:T(8,128)}, f32[256,1280]{1,0:T(8,128)S(1)}, u32[]{:S(2)}, u32[]{:S(2)}) collective-permute-start(f32[256,1280]{1,0:T(8,128)} %refs_2_.3), channel_id=1, source_target_pairs={{0,128},{128,0},{1,129},{129,1},{2,130},{130,2},{3,131},{131,3},{4... | collective-permute-start | bytes 3932168 | tf_op jit(solution)/shard_map/gather_integrals/ppermute | solution.py:44
  2.7 2.5 %mask.1 = (f32[4,9,512]{2,1,0:T(8,128)}, f32[4,9,512]{2,1,0:T(8,128)}) custom-call(s32[8]{0:T(128)} %occ_ref.1, s32[8]{0:T(128)} %vir_ref.1, s32[8,8]{1,0:T(8,128)} %mask_ref.1, f32[3,3,4096]{2,1,0:T(4,128)} %a_ref.1), custom_call_target="tpu_custom_call" | custom-call | flops 1000 | bytes 1000 | tf_op jit(solution)/shard_map/mask/pallas_call | solution.py:85
  5.2 1.6 %collective-permute-done.refs_1_ = f32[4,9,512]{2,1,0:T(8,128)S(1)} collective-permute-done((f32[4,9,512]{2,1,0:T(8,128)}, f32[4,9,512]{2,1,0:T(8,128)S(1)}, u32[]{:S(2)}, u32[]{:S(2)}) %collective-permute-start) | collective-permute-done | bytes 73760 | tf_op jit(solution)/shard_map/exchange_amplitudes/ppermute | solution.py:44
  7.7 1.7 %collective-permute-start.1 = (f32[2,9,512]{2,1,0:T(8,128)S(1)}, f32[2,9,512]{2,1,0:T(8,128)S(1)}, u32[]{:S(2)}, u32[]{:S(2)}) collective-permute-start(f32[2,9,512]{2,1,0:T(8,128)S(1)} %get-tuple-element.34), channel_id=1, source_target_pairs={{0,32},{32,0},{64,96},{96,64},{1,33},{33,1},{65,97},{97,65},{2,34}... | collective-permute-start | bytes 110600 | tf_op jit(solution)/shard_map/exchange_amplitudes/ppermute | solution.py:44
  9.4 2.9 %collective-permute-start.2 = (f32[2,9,512]{2,1,0:T(8,128)S(1)}, f32[2,9,512]{2,1,0:T(8,128)S(1)}, u32[]{:S(2)}, u32[]{:S(2)}) collective-permute-start(f32[2,9,512]{2,1,0:T(8,128)S(1)} %get-tuple-element.35), channel_id=1, source_target_pairs={{0,64},{32,96},{64,0},{96,32},{1,65},{33,97},{65,1},{97,33},{2,66}... | collective-permute-start | bytes 110600 | tf_op jit(solution)/shard_map/exchange_amplitudes/ppermute | solution.py:44
  12.5 3.3 %collective-permute-done.2.refs_2_ = f32[2,9,512]{2,1,0:T(8,128)S(1)} collective-permute-done((f32[2,9,512]{2,1,0:T(8,128)S(1)}, f32[2,9,512]{2,1,0:T(8,128)S(1)}, u32[]{:S(2)}, u32[]{:S(2)}) %collective-permute-start.2) | collective-permute-done | bytes 36896 | tf_op jit(solution)/shard_map/exchange_amplitudes/ppermute | solution.py:44
  15.8 1.9 %collective-permute-done.3.refs_3_ = f32[2,9,512]{2,1,0:T(8,128)S(1)} collective-permute-done((f32[2,9,512]{2,1,0:T(8,128)S(1)}, f32[2,9,512]{2,1,0:T(8,128)S(1)}, u32[]{:S(2)}, u32[]{:S(2)}) %collective-permute-start.3) | collective-permute-done | bytes 36896 | tf_op jit(solution)/shard_map/exchange_amplitudes/ppermute | solution.py:44
  17.8 2.0 %collective-permute-start.4 = (f32[72,512]{1,0:T(8,128)S(1)}, f32[72,512]{1,0:T(8,128)S(1)}, u32[]{:S(2)}, u32[]{:S(2)}) collective-permute-start(f32[72,512]{1,0:T(8,128)S(1)} %line_up_kernel.1.refs_0_), channel_id=1, source_target_pairs={{0,2},{2,4},{4,6},{6,8},{8,10},{10,12},{12,14},{14,0},{1,3},{3,5},... | collective-permute-start | bytes 442376 | tf_op jit(solution)/shard_map/gather_amplitudes/ppermute | solution.py:48
  19.8 4.0 %collective-permute-start.5 = (f32[72,512]{1,0:T(8,128)S(1)}, f32[72,512]{1,0:T(8,128)S(1)}, u32[]{:S(2)}, u32[]{:S(2)}) collective-permute-start(f32[72,512]{1,0:T(8,128)S(1)} %line_up_kernel.1.refs_0_), channel_id=1, source_target_pairs={{0,14},{2,0},{4,2},{6,4},{8,6},{10,8},{12,10},{14,12},{1,15},{3,1}... | collective-permute-start | bytes 442376 | tf_op jit(solution)/shard_map/gather_amplitudes/ppermute | solution.py:48
  23.8 4.6 %collective-permute-done.4.refs_0_.refs_1_ = f32[72,512]{1,0:T(8,128)S(1)} collective-permute-done((f32[72,512]{1,0:T(8,128)S(1)}, f32[72,512]{1,0:T(8,128)S(1)}, u32[]{:S(2)}, u32[]{:S(2)}) %collective-permute-start.4) | collective-permute-done | bytes 147488 | tf_op jit(solution)/shard_map/gather_amplitudes/ppermute | solution.py:48
  28.4 3.6 %collective-permute-start.7 = (f32[72,512]{1,0:T(8,128)S(1)}, f32[72,512]{1,0:T(8,128)S(1)}, u32[]{:S(2)}, u32[]{:S(2)}) collective-permute-start(f32[72,512]{1,0:T(8,128)S(1)} %line_up_kernel.1.refs_0_), channel_id=1, source_target_pairs={{0,12},{2,14},{4,0},{6,2},{8,4},{10,6},{12,8},{14,10},{1,13},{3,15... | collective-permute-start | bytes 442376 | tf_op jit(solution)/shard_map/gather_amplitudes/ppermute | solution.py:48
  32.0 1.5 %collective-permute-done.6.refs_2_.refs_3_ = f32[72,512]{1,0:T(8,128)S(1)} collective-permute-done((f32[72,512]{1,0:T(8,128)S(1)}, f32[72,512]{1,0:T(8,128)S(1)}, u32[]{:S(2)}, u32[]{:S(2)}) %collective-permute-start.6) | collective-permute-done | bytes 147488 | tf_op jit(solution)/shard_map/gather_amplitudes/ppermute | solution.py:48
  33.5 2.8 %collective-permute-done.7.refs_3_.refs_4_ = f32[72,512]{1,0:T(8,128)S(1)} collective-permute-done((f32[72,512]{1,0:T(8,128)S(1)}, f32[72,512]{1,0:T(8,128)S(1)}, u32[]{:S(2)}, u32[]{:S(2)}) %collective-permute-start.7) | collective-permute-done | bytes 147488 | tf_op jit(solution)/shard_map/gather_amplitudes/ppermute | solution.py:48
  36.5 2.9 %collective-permute-start.14 = (f32[128,1280]{1,0:T(8,128)S(1)}, f32[128,1280]{1,0:T(8,128)S(1)}, u32[]{:S(2)}, u32[]{:S(2)}) collective-permute-start(f32[128,1280]{1,0:T(8,128)S(1)} %get-tuple-element.44), channel_id=1, source_target_pairs={{0,128},{128,0},{1,129},{129,1},{2,130},{130,2},{3,131},{131,3},{4... | collective-permute-start | bytes 1966088 | tf_op jit(solution)/shard_map/gather_integrals/ppermute | solution.py:44
  39.4 3.2 %collective-permute-start.8 = (f32[112,512]{1,0:T(8,128)S(1)}, f32[112,512]{1,0:T(8,128)S(1)}, u32[]{:S(2)}, u32[]{:S(2)}) collective-permute-start(f32[112,512]{1,0:T(8,128)S(1)} %get-tuple-element.37.refs_2_), channel_id=1, source_target_pairs={{0,4},{2,6},{4,8},{6,10},{8,12},{10,14},{12,0},{14,2},{1,5},{3,7},... | collective-permute-start | bytes 688136 | tf_op jit(solution)/shard_map/gather_amplitudes/ppermute | solution.py:48
  43.9 7.6 %collective-permute-done.9.refs_6_ = f32[104,512]{1,0:T(8,128)S(1)} collective-permute-done((f32[104,512]{1,0:T(8,128)S(1)}, f32[104,512]{1,0:T(8,128)S(1)}, u32[]{:S(2)}, u32[]{:S(2)}) %collective-permute-start.9) | collective-permute-done | bytes 213024 | tf_op jit(solution)/shard_map/gather_amplitudes/ppermute | solution.py:48
  52.4 1.6 %theirs_kernel.2 = f32[288,1280]{1,0:T(8,128)S(1)} custom-call(bf16[288,512]{1,0:T(8,128)(2,1)S(1)} %get-tuple-element.41.refs_0_, bf16[288,512]{1,0:T(8,128)(2,1)S(1)} %get-tuple-element.42.refs_1_, f32[256,1280]{1,0:T(8,128)S(1)} %copy-done, f32[256,1280]{1,0:T(8,128)S(1)} %collective-permute-done.10.refs_3_.refs_0_), custom_call_target="tpu_custom_call" | custom-call | flops 1000 | bytes 1000 | tf_op jit(solution)/shard_map/product/theirs_kernel/pallas_call | solution.py:23
  54.3 1.6 %theirs_kernel.3.refs_5_ = f32[288,1280]{1,0:T(8,128)S(1)} custom-call(bf16[288,512]{1,0:T(8,128)(2,1)S(1)} %get-tuple-element.41.refs_0_, bf16[288,512]{1,0:T(8,128)(2,1)S(1)} %get-tuple-element.42.refs_1_, f32[128,1280]{1,0:T(8,128)S(1)} %collective-permute-done.13.refs_2_, f32[128,1280]{1,0:T(8,128)S(1)} %collective-permute-done.14.refs_3_, ...), custom_call_target="tpu_custom_call" | custom-call | flops 1000 | bytes 1000 | tf_op jit(solution)/shard_map/product/theirs_kernel/pallas_call | solution.py:23
  57.6 1.7 %ours_kernel.2 = (f32[144,640]{1,0:T(8,128)S(1)}, f32[144,640]{1,0:T(8,128)S(1)}, f32[144,640]{1,0:T(8,128)S(1)}, f32[144,640]{1,0:T(8,128)S(1)}) custom-call(bf16[288,512]{1,0:T(8,128)(2,1)S(1)} %get-tuple-element.39.refs_0_, bf16[288,512]{1,0:T(8,128)(2,1)S(1)} %get-tuple-element.40.refs_1_, f32[256,1280]{1,0:T(8,128)S(1)} %copy-done, ...), custom_call_target="tpu_custom_call" | custom-call | flops 1000 | bytes 1000 | tf_op jit(solution)/shard_map/product/ours_kernel/pallas_call | solution.py:23
  60.6 2.2 %collective-permute-start.16 = (f32[144,640]{1,0:T(8,128)S(1)}, f32[144,640]{1,0:T(8,128)S(1)}, u32[]{:S(2)}, u32[]{:S(2)}) collective-permute-start(f32[144,640]{1,0:T(8,128)S(1)} %get-tuple-element.48), channel_id=1, source_target_pairs={{0,96},{32,64},{64,32},{96,0},{1,97},{33,65},{65,33},{97,1},{2,98}... | collective-permute-start | bytes 1105928 | tf_op jit(solution)/shard_map/sum_y/ppermute | solution.py:44
  62.7 1.7 %ours_kernel.3 = (f32[144,640]{1,0:T(8,128)S(1)}, f32[144,640]{1,0:T(8,128)S(1)}, f32[144,640]{1,0:T(8,128)S(1)}, f32[144,640]{1,0:T(8,128)S(1)}) custom-call(bf16[288,512]{1,0:T(8,128)(2,1)S(1)} %get-tuple-element.39.refs_0_, bf16[288,512]{1,0:T(8,128)(2,1)S(1)} %get-tuple-element.40.refs_1_, f32[128,1280]{1,0:T(8,128)S(1)} %collective-permute-done.13.refs_2_, ...), custom_call_target="tpu_custom_call" | custom-call | flops 1000 | bytes 1000 | tf_op jit(solution)/shard_map/product/ours_kernel/pallas_call | solution.py:23
  65.8 5.0 %collective-permute-done.15.refs_1_ = f32[144,640]{1,0:T(8,128)S(1)} collective-permute-done((f32[144,640]{1,0:T(8,128)S(1)}, f32[144,640]{1,0:T(8,128)S(1)}, u32[]{:S(2)}, u32[]{:S(2)}) %collective-permute-start.15) | collective-permute-done | bytes 368672 | tf_op jit(solution)/shard_map/sum_y/ppermute | solution.py:44
  70.8 2.4 %collective-permute-done.16.refs_3_.refs_4_ = f32[144,640]{1,0:T(8,128)S(1)} collective-permute-done((f32[144,640]{1,0:T(8,128)S(1)}, f32[144,640]{1,0:T(8,128)S(1)}, u32[]{:S(2)}, u32[]{:S(2)}) %collective-permute-start.16) | collective-permute-done | bytes 368672 | tf_op jit(solution)/shard_map/sum_y/ppermute | solution.py:44
  73.3 2.3 %collective-permute-start.18 = (f32[72,640]{1,0:T(8,128)S(1)}, f32[72,640]{1,0:T(8,128)S(1)}, u32[]{:S(2)}, u32[]{:S(2)}) collective-permute-start(f32[72,640]{1,0:T(8,128)S(1)} %get-tuple-element.50), channel_id=1, source_target_pairs={{0,96},{32,64},{64,32},{96,0},{1,97},{33,65},{65,33},{97,1},{2,98}... | collective-permute-start | bytes 552968 | tf_op jit(solution)/shard_map/sum_y/ppermute | solution.py:44
  75.6 3.1 %collective-permute-done.20.refs_1_.refs_7_ = f32[144,640]{1,0:T(8,128)S(1)} collective-permute-done((f32[144,640]{1,0:T(8,128)S(1)}, f32[144,640]{1,0:T(8,128)S(1)}, u32[]{:S(2)}, u32[]{:S(2)}) %collective-permute-start.20) | collective-permute-done | bytes 368672 | tf_op jit(solution)/shard_map/sum_y/ppermute | solution.py:44
  78.7 2.4 %collective-permute-done.21.refs_3_.refs_10_ = f32[144,640]{1,0:T(8,128)S(1)} collective-permute-done((f32[144,640]{1,0:T(8,128)S(1)}, f32[144,640]{1,0:T(8,128)S(1)}, u32[]{:S(2)}, u32[]{:S(2)}) %collective-permute-start.21) | collective-permute-done | bytes 368672 | tf_op jit(solution)/shard_map/sum_y/ppermute | solution.py:44
  81.2 2.3 %collective-permute-start.22 = (f32[72,640]{1,0:T(8,128)S(1)}, f32[72,640]{1,0:T(8,128)S(1)}, u32[]{:S(2)}, u32[]{:S(2)}) collective-permute-start(f32[72,640]{1,0:T(8,128)S(1)} %get-tuple-element.55), channel_id=1, source_target_pairs={{0,96},{32,64},{64,32},{96,0},{1,97},{33,65},{65,33},{97,1},{2,98}... | collective-permute-start | bytes 552968 | tf_op jit(solution)/shard_map/sum_y/ppermute | solution.py:44
  83.5 1.4 %collective-permute-done.18.refs_2_ = f32[72,640]{1,0:T(8,128)S(1)} collective-permute-done((f32[72,640]{1,0:T(8,128)S(1)}, f32[72,640]{1,0:T(8,128)S(1)}, u32[]{:S(2)}, u32[]{:S(2)}) %collective-permute-start.18) | collective-permute-done | bytes 184352 | tf_op jit(solution)/shard_map/sum_y/ppermute | solution.py:44
  84.9 3.1 %collective-permute-done.22.refs_8_ = f32[72,640]{1,0:T(8,128)S(1)} collective-permute-done((f32[72,640]{1,0:T(8,128)S(1)}, f32[72,640]{1,0:T(8,128)S(1)}, u32[]{:S(2)}, u32[]{:S(2)}) %collective-permute-start.22) | collective-permute-done | bytes 184352 | tf_op jit(solution)/shard_map/sum_y/ppermute | solution.py:44
  90.0 5.6 %all-to-all-start = ((f32[8,180,128]{2,1,0:T(8,128)}), f32[8,180,128]{2,1,0:T(8,128)S(1)}, u32[]{:S(2)}, u32[]{:S(2)}) async-start(f32[8,180,128]{2,1,0:T(8,128)} %finish_kernel.1), calls=%async_computation | async-start | bytes 1507328 | tf_op jit(solution)/shard_map/to_owner/all_to_all | solution.py:312
  95.7 19.3 %all-to-all-done.refs_0_ = f32[8,180,128]{2,1,0:T(8,128)S(1)} async-done(((f32[8,180,128]{2,1,0:T(8,128)}), f32[8,180,128]{2,1,0:T(8,128)S(1)}, u32[]{:S(2)}, u32[]{:S(2)}) %all-to-all-start) | async-done | bytes 737312 | tf_op jit(solution)/shard_map/to_owner/all_to_all | solution.py:312
  115.0 1.4 %scale_kernel.1 = f32[3,3,20480]{2,1,0:T(4,128)} custom-call(f32[8,180,128]{2,1,0:T(8,128)S(1)} %all-to-all-done.refs_0_, f32[9,1]{1,0:T(8,128)S(1)} %reshape.4.refs_1_, f32[1,20480]{1,0:T(1,128)S(1)} %bitcast.1), custom_call_target="tpu_custom_call" | custom-call | flops 1000 | bytes 1000 | tf_op jit(solution)/shard_map/scale/scale_kernel/pallas_call | solution.py:23
  (41 shorter events, 10.8 us)
Async XLA Ops:
  0.0 36.3 %collective-permute-start.10 = (f32[256,1280]{1,0:T(8,128)}, f32[256,1280]{1,0:T(8,128)S(1)}, u32[]{:S(2)}, u32[]{:S(2)}) collective-permute-start(f32[256,1280]{1,0:T(8,128)} %refs_2_.3), channel_id=1, source_target_pairs={{0,128},{128,0},{1,129},{129,1},{2,130},{130,2},{3,131},{131,3},{4... | collective-permute-start | bytes 3932168 | tf_op jit(solution)/shard_map/gather_integrals/ppermute | solution.py:44
  2.3 34.0 %collective-permute-start.12 = (f32[256,1280]{1,0:T(8,128)}, f32[256,1280]{1,0:T(8,128)S(1)}, u32[]{:S(2)}, u32[]{:S(2)}) collective-permute-start(f32[256,1280]{1,0:T(8,128)} %refs_2_.3), channel_id=1, source_target_pairs={{0,129},{1,128},{128,1},{129,0},{2,131},{3,130},{130,3},{131,2},{4... | collective-permute-start | bytes 3932168 | tf_op jit(solution)/shard_map/gather_integrals/ppermute | solution.py:44
  5.2 1.6 %collective-permute-start = (f32[4,9,512]{2,1,0:T(8,128)}, f32[4,9,512]{2,1,0:T(8,128)S(1)}, u32[]{:S(2)}, u32[]{:S(2)}) collective-permute-start(f32[4,9,512]{2,1,0:T(8,128)} %get-tuple-element.32), channel_id=1, source_target_pairs={{0,16},{16,0},{1,17},{17,1},{2,18},{18,2},{3,19},{19,3},{4,20},{20... | collective-permute-start | bytes 221192 | tf_op jit(solution)/shard_map/exchange_amplitudes/ppermute | solution.py:44
  6.8 0.9 copy-start.1
  7.7 4.8 %collective-permute-start.1 = (f32[2,9,512]{2,1,0:T(8,128)S(1)}, f32[2,9,512]{2,1,0:T(8,128)S(1)}, u32[]{:S(2)}, u32[]{:S(2)}) collective-permute-start(f32[2,9,512]{2,1,0:T(8,128)S(1)} %get-tuple-element.34), channel_id=1, source_target_pairs={{0,32},{32,0},{64,96},{96,64},{1,33},{33,1},{65,97},{97,65},{2,34}... | collective-permute-start | bytes 110600 | tf_op jit(solution)/shard_map/exchange_amplitudes/ppermute | solution.py:44
  9.4 6.4 %collective-permute-start.2 = (f32[2,9,512]{2,1,0:T(8,128)S(1)}, f32[2,9,512]{2,1,0:T(8,128)S(1)}, u32[]{:S(2)}, u32[]{:S(2)}) collective-permute-start(f32[2,9,512]{2,1,0:T(8,128)S(1)} %get-tuple-element.35), channel_id=1, source_target_pairs={{0,64},{32,96},{64,0},{96,32},{1,65},{33,97},{65,1},{97,33},{2,66}... | collective-permute-start | bytes 110600 | tf_op jit(solution)/shard_map/exchange_amplitudes/ppermute | solution.py:44
  12.3 5.5 %collective-permute-start.3 = (f32[2,9,512]{2,1,0:T(8,128)S(1)}, f32[2,9,512]{2,1,0:T(8,128)S(1)}, u32[]{:S(2)}, u32[]{:S(2)}) collective-permute-start(f32[2,9,512]{2,1,0:T(8,128)S(1)} %get-tuple-element.36), channel_id=1, source_target_pairs={{0,96},{32,64},{64,32},{96,0},{1,97},{33,65},{65,33},{97,1},{2,98}... | collective-permute-start | bytes 110600 | tf_op jit(solution)/shard_map/exchange_amplitudes/ppermute | solution.py:44
  17.8 10.6 %collective-permute-start.4 = (f32[72,512]{1,0:T(8,128)S(1)}, f32[72,512]{1,0:T(8,128)S(1)}, u32[]{:S(2)}, u32[]{:S(2)}) collective-permute-start(f32[72,512]{1,0:T(8,128)S(1)} %line_up_kernel.1.refs_0_), channel_id=1, source_target_pairs={{0,2},{2,4},{4,6},{6,8},{8,10},{10,12},{12,14},{14,0},{1,3},{3,5},... | collective-permute-start | bytes 442376 | tf_op jit(solution)/shard_map/gather_amplitudes/ppermute | solution.py:48
  19.8 12.2 %collective-permute-start.5 = (f32[72,512]{1,0:T(8,128)S(1)}, f32[72,512]{1,0:T(8,128)S(1)}, u32[]{:S(2)}, u32[]{:S(2)}) collective-permute-start(f32[72,512]{1,0:T(8,128)S(1)} %line_up_kernel.1.refs_0_), channel_id=1, source_target_pairs={{0,14},{2,0},{4,2},{6,4},{8,6},{10,8},{12,10},{14,12},{1,15},{3,1}... | collective-permute-start | bytes 442376 | tf_op jit(solution)/shard_map/gather_amplitudes/ppermute | solution.py:48
  23.8 9.7 %collective-permute-start.6 = (f32[72,512]{1,0:T(8,128)S(1)}, f32[72,512]{1,0:T(8,128)S(1)}, u32[]{:S(2)}, u32[]{:S(2)}) collective-permute-start(f32[72,512]{1,0:T(8,128)S(1)} %line_up_kernel.1.refs_0_), channel_id=1, source_target_pairs={{0,4},{2,6},{4,8},{6,10},{8,12},{10,14},{12,0},{14,2},{1,5},{3,7},... | collective-permute-start | bytes 442376 | tf_op jit(solution)/shard_map/gather_amplitudes/ppermute | solution.py:48
  28.4 7.8 %collective-permute-start.7 = (f32[72,512]{1,0:T(8,128)S(1)}, f32[72,512]{1,0:T(8,128)S(1)}, u32[]{:S(2)}, u32[]{:S(2)}) collective-permute-start(f32[72,512]{1,0:T(8,128)S(1)} %line_up_kernel.1.refs_0_), channel_id=1, source_target_pairs={{0,12},{2,14},{4,0},{6,2},{8,4},{10,6},{12,8},{14,10},{1,13},{3,15... | collective-permute-start | bytes 442376 | tf_op jit(solution)/shard_map/gather_amplitudes/ppermute | solution.py:48
  36.3 16.1 %copy-start = (f32[256,1280]{1,0:T(8,128)S(1)}, f32[256,1280]{1,0:T(8,128)}, u32[]{:S(2)}) copy-start(f32[256,1280]{1,0:T(8,128)} %refs_2_.3) | copy-start | bytes 3932164
  36.4 17.9 %collective-permute-start.13 = (f32[128,1280]{1,0:T(8,128)S(1)}, f32[128,1280]{1,0:T(8,128)S(1)}, u32[]{:S(2)}, u32[]{:S(2)}) collective-permute-start(f32[128,1280]{1,0:T(8,128)S(1)} %get-tuple-element.43), channel_id=1, source_target_pairs={{0,129},{1,128},{128,1},{129,0},{2,131},{3,130},{130,3},{131,2},{4... | collective-permute-start | bytes 1966088 | tf_op jit(solution)/shard_map/gather_integrals/ppermute | solution.py:44
  36.5 17.8 %collective-permute-start.14 = (f32[128,1280]{1,0:T(8,128)S(1)}, f32[128,1280]{1,0:T(8,128)S(1)}, u32[]{:S(2)}, u32[]{:S(2)}) collective-permute-start(f32[128,1280]{1,0:T(8,128)S(1)} %get-tuple-element.44), channel_id=1, source_target_pairs={{0,128},{128,0},{1,129},{129,1},{2,130},{130,2},{3,131},{131,3},{4... | collective-permute-start | bytes 1966088 | tf_op jit(solution)/shard_map/gather_integrals/ppermute | solution.py:44
  39.4 12.6 %collective-permute-start.8 = (f32[112,512]{1,0:T(8,128)S(1)}, f32[112,512]{1,0:T(8,128)S(1)}, u32[]{:S(2)}, u32[]{:S(2)}) collective-permute-start(f32[112,512]{1,0:T(8,128)S(1)} %get-tuple-element.37.refs_2_), channel_id=1, source_target_pairs={{0,4},{2,6},{4,8},{6,10},{8,12},{10,14},{12,0},{14,2},{1,5},{3,7},... | collective-permute-start | bytes 688136 | tf_op jit(solution)/shard_map/gather_amplitudes/ppermute | solution.py:48
  42.6 9.0 %collective-permute-start.9 = (f32[104,512]{1,0:T(8,128)S(1)}, f32[104,512]{1,0:T(8,128)S(1)}, u32[]{:S(2)}, u32[]{:S(2)}) collective-permute-start(f32[104,512]{1,0:T(8,128)S(1)} %get-tuple-element.38), channel_id=1, source_target_pairs={{0,12},{2,14},{4,0},{6,2},{8,4},{10,6},{12,8},{14,10},{1,13},{3,15... | collective-permute-start | bytes 638984 | tf_op jit(solution)/shard_map/gather_amplitudes/ppermute | solution.py:48
  54.0 3.5 %collective-permute-start.11 = (f32[288,1280]{1,0:T(8,128)S(1)}, f32[288,1280]{1,0:T(8,128)S(1)}, u32[]{:S(2)}, u32[]{:S(2)}) collective-permute-start(f32[288,1280]{1,0:T(8,128)S(1)} %theirs_kernel.2), channel_id=1, source_target_pairs={{0,16},{16,0},{1,17},{17,1},{2,18},{18,2},{3,19},{19,3},{4,20},{20... | collective-permute-start | bytes 4423688 | tf_op jit(solution)/shard_map/sum_core/ppermute | solution.py:44
  56.0 6.8 %collective-permute-start.17 = (f32[288,1280]{1,0:T(8,128)S(1)}, f32[288,1280]{1,0:T(8,128)S(1)}, u32[]{:S(2)}, u32[]{:S(2)}) collective-permute-start(f32[288,1280]{1,0:T(8,128)S(1)} %theirs_kernel.3.refs_5_), channel_id=1, source_target_pairs={{0,16},{16,0},{1,17},{17,1},{2,18},{18,2},{3,19},{19,3},{4,20},{20... | collective-permute-start | bytes 4423688 | tf_op jit(solution)/shard_map/sum_core/ppermute | solution.py:44
  59.3 11.5 %collective-permute-start.15 = (f32[144,640]{1,0:T(8,128)S(1)}, f32[144,640]{1,0:T(8,128)S(1)}, u32[]{:S(2)}, u32[]{:S(2)}) collective-permute-start(f32[144,640]{1,0:T(8,128)S(1)} %get-tuple-element.46), channel_id=1, source_target_pairs={{0,32},{32,0},{64,96},{96,64},{1,33},{33,1},{65,97},{97,65},{2,34}... | collective-permute-start | bytes 1105928 | tf_op jit(solution)/shard_map/sum_y/ppermute | solution.py:44
  60.6 12.7 %collective-permute-start.16 = (f32[144,640]{1,0:T(8,128)S(1)}, f32[144,640]{1,0:T(8,128)S(1)}, u32[]{:S(2)}, u32[]{:S(2)}) collective-permute-start(f32[144,640]{1,0:T(8,128)S(1)} %get-tuple-element.48), channel_id=1, source_target_pairs={{0,96},{32,64},{64,32},{96,0},{1,97},{33,65},{65,33},{97,1},{2,98}... | collective-permute-start | bytes 1105928 | tf_op jit(solution)/shard_map/sum_y/ppermute | solution.py:44
  64.5 14.3 %collective-permute-start.20 = (f32[144,640]{1,0:T(8,128)S(1)}, f32[144,640]{1,0:T(8,128)S(1)}, u32[]{:S(2)}, u32[]{:S(2)}) collective-permute-start(f32[144,640]{1,0:T(8,128)S(1)} %get-tuple-element.49.refs_4_), channel_id=1, source_target_pairs={{0,32},{32,0},{64,96},{96,64},{1,33},{33,1},{65,97},{97,65},{2,34}... | collective-permute-start | bytes 1105928 | tf_op jit(solution)/shard_map/sum_y/ppermute | solution.py:44
  65.2 15.9 %collective-permute-start.21 = (f32[144,640]{1,0:T(8,128)S(1)}, f32[144,640]{1,0:T(8,128)S(1)}, u32[]{:S(2)}, u32[]{:S(2)}) collective-permute-start(f32[144,640]{1,0:T(8,128)S(1)} %get-tuple-element.54), channel_id=1, source_target_pairs={{0,96},{32,64},{64,32},{96,0},{1,97},{33,65},{65,33},{97,1},{2,98}... | collective-permute-start | bytes 1105928 | tf_op jit(solution)/shard_map/sum_y/ppermute | solution.py:44
  73.3 11.6 %collective-permute-start.18 = (f32[72,640]{1,0:T(8,128)S(1)}, f32[72,640]{1,0:T(8,128)S(1)}, u32[]{:S(2)}, u32[]{:S(2)}) collective-permute-start(f32[72,640]{1,0:T(8,128)S(1)} %get-tuple-element.50), channel_id=1, source_target_pairs={{0,96},{32,64},{64,32},{96,0},{1,97},{33,65},{65,33},{97,1},{2,98}... | collective-permute-start | bytes 552968 | tf_op jit(solution)/shard_map/sum_y/ppermute | solution.py:44
  75.6 9.4 %collective-permute-start.19 = (f32[72,640]{1,0:T(8,128)S(1)}, f32[72,640]{1,0:T(8,128)S(1)}, u32[]{:S(2)}, u32[]{:S(2)}) collective-permute-start(f32[72,640]{1,0:T(8,128)S(1)} %get-tuple-element.51), channel_id=1, source_target_pairs={{0,32},{32,0},{64,96},{96,64},{1,33},{33,1},{65,97},{97,65},{2,34}... | collective-permute-start | bytes 552968 | tf_op jit(solution)/shard_map/sum_y/ppermute | solution.py:44
  81.2 6.8 %collective-permute-start.22 = (f32[72,640]{1,0:T(8,128)S(1)}, f32[72,640]{1,0:T(8,128)S(1)}, u32[]{:S(2)}, u32[]{:S(2)}) collective-permute-start(f32[72,640]{1,0:T(8,128)S(1)} %get-tuple-element.55), channel_id=1, source_target_pairs={{0,96},{32,64},{64,32},{96,0},{1,97},{33,65},{65,33},{97,1},{2,98}... | collective-permute-start | bytes 552968 | tf_op jit(solution)/shard_map/sum_y/ppermute | solution.py:44
  83.5 5.5 %collective-permute-start.23 = (f32[72,640]{1,0:T(8,128)S(1)}, f32[72,640]{1,0:T(8,128)S(1)}, u32[]{:S(2)}, u32[]{:S(2)}) collective-permute-start(f32[72,640]{1,0:T(8,128)S(1)} %get-tuple-element.56), channel_id=1, source_target_pairs={{0,32},{32,0},{64,96},{96,64},{1,33},{33,1},{65,97},{97,65},{2,34}... | collective-permute-start | bytes 552968 | tf_op jit(solution)/shard_map/sum_y/ppermute | solution.py:44
  90.0 5.6 %copy-start.3 = (f32[3,3]{1,0:T(4,128)S(1)}, f32[3,3]{1,0:T(4,128)}, u32[]{:S(2)}) copy-start(f32[3,3]{1,0:T(4,128)} %param.12) | copy-start | bytes 112
  90.0 25.0 %copy-start.2 = (f32[20480]{0:T(1024)S(1)}, f32[20480]{0:T(1024)}, u32[]{:S(2)}) copy-start(f32[20480]{0:T(1024)} %param.13) | copy-start | bytes 245764
  90.0 25.0 %all-to-all-start = ((f32[8,180,128]{2,1,0:T(8,128)}), f32[8,180,128]{2,1,0:T(8,128)S(1)}, u32[]{:S(2)}, u32[]{:S(2)}) async-start(f32[8,180,128]{2,1,0:T(8,128)} %finish_kernel.1), calls=%async_computation | async-start | bytes 1507328 | tf_op jit(solution)/shard_map/to_owner/all_to_all | solution.py:312
